TPU v7x, 512 devices: a whole 4x4x16 slice. The times are simulated.
512 devices in a mesh: dp: 32 (over y_lo, z), mp: 16 (over x, y_hi, core).
Axes of the slice: x: 4, y: 4 (y_hi: 2, y_lo: 2; y = y_hi * 2 + y_lo), z: 16, core: 2. Of those that a mesh axis runs over, the one named last changes fastest.
Arguments:
- activations: bfloat16 [49152, 18432], P('dp', 'mp'), may hold values from -6 to 6
- cotangent: bfloat16 [49152, 3072], P('dp', 'mp'), may hold values from -0.03125 to 0.03125
- resident_key_value_weight: bfloat16 [18432, 3072], P('dp', 'mp'), may hold values from -0.75 to 0.75
- down_master: float32 [16, 1152, 128], P('mp', 'dp'), may hold values from -0.75 to 0.75
- down_first: float32 [16, 1152, 128], P('mp', 'dp'), may hold values from -6 to 6
- down_second: float32 [16, 1152, 128], P('mp', 'dp'), may hold values from 1 to 50
- up_master: float32 [16, 192, 128], P('mp', 'dp'), may hold values from -0.75 to 0.75
- up_first: float32 [16, 192, 128], P('mp', 'dp'), may hold values from -6 to 6
- up_second: float32 [16, 192, 128], P('mp', 'dp'), may hold values from 1 to 50
Outputs:
- merged_key_value_weight: bfloat16 [18432, 3072], P('dp', 'mp')
- down_master_new: float32 [16, 1152, 128], P('mp', 'dp')
- down_first_new: float32 [16, 1152, 128], P('mp', 'dp')
- down_second_new: float32 [16, 1152, 128], P('mp', 'dp')
- up_master_new: float32 [16, 192, 128], P('mp', 'dp')
- up_first_new: float32 [16, 192, 128], P('mp', 'dp')
- up_second_new: float32 [16, 192, 128], P('mp', 'dp')
All inputs are finite; a program needn't handle non-finite values.
Results may differ from a plain program's by a relative error of at most 0.013.
Values may be sent and summed in bfloat16 or wider, within the bound.
No kernel may reach another device: no remote copies, remote signals or barrier semaphores. Data moves between devices by JAX's collectives and lax.ppermute only.
A program may use at most 64 MiB of HBM per device.

v0:
```python
import jax
import jax.numpy as jnp
from jax import lax
from jax.sharding import PartitionSpec as P

adapter_scale_factor = 2.0
learn_rate = 0.05
beta_one = 0.9
beta_two = 0.999
adam_eps = 1e-08
decay_rate = 0.01
step_count = 10.0


def adamw_update(master, first, second, grad):
    first_new = beta_one * first + (1.0 - beta_one) * grad
    second_new = beta_two * second + (1.0 - beta_two) * grad * grad
    first_hat = first_new / (1.0 - beta_one**step_count)
    second_hat = second_new / (1.0 - beta_two**step_count)
    master_new = master - learn_rate * (
        first_hat / (jnp.sqrt(second_hat) + adam_eps) + decay_rate * master
    )
    return (master_new, first_new, second_new)


def token_contraction_sum(left, right):
    return lax.dot_general(
        left, right, (((0,), (0,)), ((), ())), preferred_element_type=jnp.float32
    )


def shards(
    activations,
    cotangent,
    resident_key_value_weight,
    down_master,
    down_first,
    down_second,
    up_master,
    up_first,
    up_second,
):
    down_half = down_master[0].astype(jnp.bfloat16)
    up_half = up_master[0].astype(jnp.bfloat16)
    a_use, bt_use = (
        lax.all_gather(down_half, "dp", axis=0, tiled=True),
        lax.all_gather(up_half, "dp", axis=0, tiled=True),
    )
    hidden_part = jnp.dot(activations, a_use, preferred_element_type=jnp.float32)
    back_part = jnp.dot(cotangent, bt_use, preferred_element_type=jnp.float32)
    hidden, back = (
        lax.psum(hidden_part.astype(jnp.bfloat16), "mp").astype(jnp.float32),
        lax.psum(back_part.astype(jnp.bfloat16), "mp").astype(jnp.float32),
    )
    hidden_activation16 = hidden.astype(jnp.bfloat16)
    backward_half_precision16 = back.astype(jnp.bfloat16)
    down_projection_term = adapter_scale_factor * token_contraction_sum(
        activations, backward_half_precision16
    )
    up_projection_term = adapter_scale_factor * token_contraction_sum(
        cotangent, hidden_activation16
    )
    down_gradient_matrix, up_gradient_matrix = (
        lax.psum_scatter(
            down_projection_term.astype(jnp.bfloat16), "dp", scatter_dimension=0, tiled=True
        ).astype(jnp.float32),
        lax.psum_scatter(
            up_projection_term.astype(jnp.bfloat16), "dp", scatter_dimension=0, tiled=True
        ).astype(jnp.float32),
    )
    down_new = adamw_update(down_master, down_first, down_second, down_gradient_matrix[None])
    up_new = adamw_update(up_master, up_first, up_second, up_gradient_matrix[None])
    down_send = down_new[0][0].astype(jnp.bfloat16)
    up_send = up_new[0][0].astype(jnp.bfloat16)
    data_count = lax.axis_size("dp")
    model_count = lax.axis_size("mp")
    group_ratio = data_count // model_count
    data_index = lax.axis_index("dp")
    model_index = lax.axis_index("mp")
    every_down, every_up = (
        lax.all_gather(down_send, ("dp", "mp"), axis=0, tiled=True),
        lax.all_gather(up_send, ("dp", "mp"), axis=0, tiled=True),
    )
    shard_down = down_send.shape[0]
    shard_up = up_send.shape[0]
    rank_width = down_send.shape[1]
    down_grid = every_down.reshape(data_count, model_count, shard_down, rank_width)
    down_pick = lax.dynamic_index_in_dim(down_grid, data_index // group_ratio, 1, keepdims=False)
    down_pick = lax.dynamic_slice_in_dim(
        down_pick, data_index % group_ratio * model_count, model_count, 0
    )
    a_rows = down_pick.reshape(model_count * shard_down, rank_width)
    up_grid = every_up.reshape(data_count, model_count, shard_up, rank_width)
    bt_rows = lax.dynamic_index_in_dim(up_grid, model_index, 1, keepdims=False).reshape(
        data_count * shard_up, rank_width
    )
    adapter_difference = lax.dot_general(
        a_rows, bt_rows, (((1,), (1,)), ((), ())), preferred_element_type=jnp.float32
    )
    merged_key_value_weight = (
        resident_key_value_weight.astype(jnp.float32) + adapter_scale_factor * adapter_difference
    ).astype(jnp.bfloat16)
    return (
        merged_key_value_weight,
        down_new[0],
        down_new[1],
        down_new[2],
        up_new[0],
        up_new[1],
        up_new[2],
    )


def solution(mesh):
    in_specs = (
        P("dp", "mp"),
        P("dp", "mp"),
        P("dp", "mp"),
        P("mp", "dp", None),
        P("mp", "dp", None),
        P("mp", "dp", None),
        P("mp", "dp", None),
        P("mp", "dp", None),
        P("mp", "dp", None),
    )
    out_specs = (
        P("dp", "mp"),
        P("mp", "dp", None),
        P("mp", "dp", None),
        P("mp", "dp", None),
        P("mp", "dp", None),
        P("mp", "dp", None),
        P("mp", "dp", None),
    )
    return jax.shard_map(shards, mesh=mesh, in_specs=in_specs, out_specs=out_specs, check_vma=False)
```

profile of v0, /device:TPU:1, one launch (start us, length us, event | category | flops | bytes accessed | tf_op | source)
XLA Modules:
  0.0 1543.9 jit_solution(2766797786472481359)
XLA Ops:
  7.2 0.8 convert_element_type.59
  8.1 56.4 %all-gather = bf16[1,192,128]{2,0,1:T(2,128)(2,1)S(1)} all-gather(bf16[1,6,128]{2,0,1:T(2,128)(2,1)S(1)} %convert_element_type.59), channel_id=2, replica_groups=mesh['dp'=32,'mp'=16] {'dp'}, dimensions={1}, use_global_device_ids=true | all-gather | bytes 50688 | tf_op jit(solution)/shard_map/all_gather | solution.py:47
  64.4 0.7 convert_element_type.67
  65.2 47.9 %all-gather.2 = bf16[1,1152,128]{2,0,1:T(2,128)(2,1)S(1)} all-gather(bf16[1,36,128]{2,0,1:T(2,128)(2,1)S(1)} %convert_element_type.67), channel_id=4, replica_groups=mesh['dp'=32,'mp'=16] {'dp'}, dimensions={1}, use_global_device_ids=true | all-gather | bytes 304128 | tf_op jit(solution)/shard_map/all_gather | solution.py:46
  113.1 2.2 convolution_convert_fusion.1
  115.3 1.8 convolution_convert_fusion
  117.2 175.5 %all-reduce.8.cloned.1.call-done = (bf16[1536,128]{1,0:T(8,128)(2,1)}, bf16[1536,128]{1,0:T(8,128)(2,1)}) async-done(((bf16[1536,128]{1,0:T(8,128)(2,1)}, bf16[1536,128]{1,0:T(8,128)(2,1)}), (bf16[1536,128]{1,0:T(8,128)(2,1)}, bf16[1536,128]{1,0:T(8,128)(2,1)})) %all-reduce.8.cloned.1.call-update) | async-done | bytes 786448 | tf_op jit(solution)/shard_map/psum | solution.py:53
  292.7 2.4 fusion.1
  295.2 1.5 copy.64
  296.6 1.5 copy.61
  298.1 1.4 copy.62
  299.6 1.3 dynamic-slice.2
  301.5 220.4 %all-reduce.6.cloned.1.call-done = bf16[1152,128]{0,1:T(8,128)(2,1)} async-done(((bf16[1152,128]{0,1:T(8,128)(2,1)}), bf16[1152,128]{0,1:T(8,128)(2,1)}) %all-reduce.6.cloned.1.call-update) | async-done | bytes 294928
  521.9 1.7 fusion.23
  523.6 1.5 copy.65
  525.8 2.1 fusion.5
  527.9 92.0 %all-reduce.1 = bf16[192,128]{1,0:T(8,128)(2,1)} all-reduce(bf16[192,128]{1,0:T(8,128)(2,1)} %fusion.5), channel_id=7, replica_groups=mesh['dp'=32,'mp'=16] {'dp'}, use_global_device_ids=true, to_apply=%region_3.0.clone | all-reduce | flops 24576 | bytes 98304
  620.0 0.7 fusion.20
  620.7 772.5 %all-gather.3 = bf16[1,3072,128]{2,0,1:T(2,128)(2,1)} all-gather(bf16[1,6,128]{2,0,1:T(2,128)(2,1)S(1)} %copy.70), channel_id=5, replica_groups=mesh['dp'=32,'mp'=16] {'dp','mp'}, dimensions={1}, use_global_device_ids=true | all-gather | bytes 787968 | tf_op jit(solution)/shard_map/all_gather | solution.py:82
  1393.2 18.4 %reduce.1 = bf16[3072,128]{1,0:T(8,128)(2,1)} reduce(bf16[1,3072,128]{2,0,1:T(2,128)(2,1)} %all-gather.3, bf16[]{:T(256)} %constant.116), dimensions={0}, to_apply=%all-gather.3.reduce_sub_computation | reduce | bytes 1572866 | tf_op jit(solution)/shard_map/all_gather | solution.py:82
  1411.6 2.1 reshape.41
  1413.7 1.5 constant_dynamic-slice_fusion
  1415.2 1.5 reshape.42
  1417.8 0.6 copy.76
  1418.4 1.5 copy.71
  1420.0 1.5 copy.72
  1421.5 1.5 copy.73
  1423.0 101.2 %reduce = bf16[18432,128]{1,0:T(8,128)(2,1)} reduce(bf16[1,18432,128]{2,0,1:T(2,128)(2,1)} %all-gather.6.cloned.1.call-done, bf16[]{:T(256)} %constant.116), dimensions={0}, to_apply=%all-gather.1.reduce_sub_computation | reduce | bytes 9437186 | tf_op jit(solution)/shard_map/all_gather | solution.py:81
  1524.2 8.0 reshape.39
  1532.2 1.6 constant_dynamic-slice_fusion.1
  1533.8 1.6 reshape.40
  1535.4 2.0 fusion.3
  (14 shorter events, 1.4 us)
Async XLA Ops:
  7.2 108.1 %copy-start = (bf16[1536,1152]{1,0:T(8,128)(2,1)S(1)}, bf16[1536,1152]{1,0:T(8,128)(2,1)}, u32[]{:S(2)}) copy-start(bf16[1536,1152]{1,0:T(8,128)(2,1)} %param.9) | copy-start | bytes 10616836
  7.2 285.5 %all-reduce.8.cloned.1.call-start = ((), (), s32[]{:S(2)}) async-start(), calls=%async_computation.2 | async-start | bytes 1572864 | tf_op jit(solution)/shard_map/psum | solution.py:53
  117.2 502.8 %copy-start.1 = (f32[1,6,128]{2,0,1:T(1,128)S(1)}, f32[1,6,128]{2,0,1:T(1,128)}, u32[]{:S(2)}) copy-start(f32[1,6,128]{2,0,1:T(1,128)} %param.15) | copy-start | bytes 9220
  117.2 404.7 %all-reduce.6.cloned.1.call-start = ((), (), s32[]{:S(2)}) async-start(), calls=%async_computation.1 | async-start | bytes 589824
  295.1 1127.9 %all-gather.6.cloned.1.call-start = ((), (), s32[]{:S(2)}) async-start(), calls=%async_computation | async-start | bytes 9455616 | tf_op jit(solution)/shard_map/all_gather | solution.py:81
Sparse Core Ops, SparseCore 0:
  117.3 175.3 all-reduce.7
  295.9 226.0 all-reduce.5
  525.3 840.4 all-gather.5
where the time goes:
time: 1560 us; the launch traced here: 1540 us
  blocking collectives  969 us (62%)
  waiting for transfers between devices  396 us (25%)
  other arithmetic  124 us (8%)
  local copies, waits for them, and re-layouts  29.7 us (2%)
    all_gather x1, blocking collectives, shards(): lax.all_gather(up_send, ('dp', 'mp'), axis=0, tiled=True)  772 us
    unnamed x4, waiting for transfers between devices  220 us
    psum x1, waiting for transfers between devices, shards(): lax.psum(back_part.astype(jnp.bfloat16), 'mp').astype(jnp.float32)  175 us
    all_gather x1, other arithmetic, shards(): lax.all_gather(down_send, ('dp', 'mp'), axis=0, tiled=True)  101 us
    unnamed x1, blocking collectives  92 us
    all_gather x1, blocking collectives, shards(): lax.all_gather(up_half, 'dp', axis=0, tiled=True)  56.4 us
    all_gather x1, blocking collectives, shards(): lax.all_gather(down_half, 'dp', axis=0, tiled=True)  47.9 us
  transfers between devices with their start and end apart: 3, of which 2 were waited for; matrix products, arithmetic and copies ran while one was open for 2% of the time, Pallas kernels for 0%

commit v1 on v0

v1 whole, which is shorter than its diff:
```python
import jax
import jax.numpy as jnp
from jax import lax
from jax.experimental import pallas as pl
from jax.experimental.pallas import tpu as pltpu
from jax.sharding import Mesh
from jax.sharding import PartitionSpec as P

adapter_scale_factor = 2.0
learn_rate = 0.05
beta_one = 0.9
beta_two = 0.999
adam_eps = 1e-08
decay_rate = 0.01
step_count = 10.0

BF = jnp.bfloat16
F32 = jnp.float32
DOWN, UP, UP_AT, SLOT = 36, 6, 40, 48
N_YL, N_Z, N_MP = 2, 16, 16
N_DP = N_YL * N_Z
RANK = 128

VMEM = pl.BlockSpec(memory_space=pltpu.VMEM)
SMEM = pl.BlockSpec(memory_space=pltpu.SMEM)


def adamw_update(master, first, second, grad):
    first_new = beta_one * first + (1.0 - beta_one) * grad
    second_new = beta_two * second + (1.0 - beta_two) * grad * grad
    first_hat = first_new / (1.0 - beta_one**step_count)
    second_hat = second_new / (1.0 - beta_two**step_count)
    master_new = master - learn_rate * (
        first_hat / (jnp.sqrt(second_hat) + adam_eps) + decay_rate * master
    )
    return (master_new, first_new, second_new)


def kernel_call(body, out_shape, n_in, scratch=(), smem=(), limit=32 * 2**20):
    many = isinstance(out_shape, (list, tuple))
    return pl.pallas_call(
        body,
        out_shape=out_shape,
        in_specs=[SMEM if i in smem else VMEM for i in range(n_in)],
        out_specs=[VMEM] * len(out_shape) if many else VMEM,
        scratch_shapes=list(scratch),
        compiler_params=pltpu.CompilerParams(vmem_limit_bytes=limit),
    )


def spread_factors(down_ref, up_ref, out_ref, slot):
    slot[...] = jnp.zeros_like(slot)
    slot[0:DOWN, :] = down_ref[0]
    slot[UP_AT : UP_AT + UP, :] = up_ref[0]
    value = slot[...].astype(BF)
    for j in range(out_ref.shape[0]):
        out_ref[j] = value


def project(slots_ref, act_ref, cot_ref, out_ref, down, up):
    for j in range(N_DP):
        value = slots_ref[j].astype(F32)
        down[j * DOWN : j * DOWN + DOWN, :] = value[0:DOWN]
        up[j * UP : j * UP + UP, :] = value[UP_AT : UP_AT + UP]
    a_use = down[...].astype(BF)
    bt_use = up[...].astype(BF)
    rows = out_ref.shape[1]
    step = 4
    for i in range(0, N_MP, step):
        at = pl.ds(i * rows, step * rows)
        hidden = jnp.dot(act_ref[at, :], a_use, preferred_element_type=F32)
        back = jnp.dot(cot_ref[at, :], bt_use, preferred_element_type=F32)
        out_ref[i : i + step, :, 0:RANK] = hidden.astype(BF).reshape(step, rows, RANK)
        out_ref[i : i + step, :, RANK:] = back.astype(BF).reshape(step, rows, RANK)


def add_parts(parts_ref, out_ref):
    total = parts_ref[0].astype(F32)
    for j in range(1, parts_ref.shape[0]):
        total += parts_ref[j].astype(F32)
    value = total.astype(BF)
    for j in range(out_ref.shape[0]):
        out_ref[j] = value


def gradients(full_ref, act_ref, cot_ref, out_ref, down, up, slot):
    tokens = act_ref.shape[0]
    full = full_ref[...].reshape(tokens, 2 * RANK)
    over_tokens = (((0,), (0,)), ((), ()))
    hidden, back = full[:, 0:RANK], full[:, RANK:]
    down[...] = adapter_scale_factor * lax.dot_general(
        act_ref[...], back, over_tokens, preferred_element_type=F32
    )
    up[...] = adapter_scale_factor * lax.dot_general(
        cot_ref[...], hidden, over_tokens, preferred_element_type=F32
    )
    slot[...] = jnp.zeros_like(slot)
    for j in range(N_DP):
        slot[0:DOWN, :] = down[j * DOWN : j * DOWN + DOWN, :]
        slot[UP_AT : UP_AT + UP, :] = up[j * UP : j * UP + UP, :]
        out_ref[j] = slot[...].astype(BF)


def update(
    parts_ref, dm_ref, df_ref, ds_ref, um_ref, uf_ref, us_ref,
    dm_out, df_out, ds_out, um_out, uf_out, us_out, send_out, slot,
):
    total = parts_ref[0].astype(F32)
    for j in range(1, parts_ref.shape[0]):
        total += parts_ref[j].astype(F32)
    down_new = adamw_update(dm_ref[0], df_ref[0], ds_ref[0], total[0:DOWN])
    up_new = adamw_update(um_ref[0], uf_ref[0], us_ref[0], total[UP_AT : UP_AT + UP])
    dm_out[0], df_out[0], ds_out[0] = down_new
    um_out[0], uf_out[0], us_out[0] = up_new
    slot[...] = jnp.zeros_like(slot)
    slot[0:DOWN, :] = down_new[0]
    slot[UP_AT : UP_AT + UP, :] = up_new[0]
    value = slot[...].astype(BF)
    for j in range(send_out.shape[0]):
        send_out[j] = value


def route(place_ref, plane_ref, out_ref, slot):
    y_lo, mp = place_ref[0], place_ref[1]
    low = plane_ref[mp].astype(F32)
    high = plane_ref[N_MP + mp].astype(F32)
    slot[DOWN : DOWN + UP, :] = low[UP_AT : UP_AT + UP]
    slot[DOWN + UP : DOWN + 2 * UP, :] = high[UP_AT : UP_AT + UP]
    for z_to in range(N_Z):
        owner = (z_to % 2) * N_MP + y_lo * (N_MP // 2) + z_to // 2
        slot[0:DOWN, :] = plane_ref[owner].astype(F32)[0:DOWN]
        out_ref[z_to] = slot[...].astype(BF)


def merge(slots_ref, base_ref, out_ref, down, up):
    half = N_Z * UP
    for z in range(N_Z):
        value = slots_ref[z].astype(F32)
        down[z * DOWN : z * DOWN + DOWN, :] = value[0:DOWN]
        up[z * UP : z * UP + UP, :] = value[DOWN : DOWN + UP]
        up[half + z * UP : half + z * UP + UP, :] = value[DOWN + UP : DOWN + 2 * UP]
    difference = lax.dot_general(
        down[...].astype(BF),
        up[...].astype(BF),
        (((1,), (1,)), ((), ())),
        preferred_element_type=F32,
    )
    out_ref[...] = (base_ref[...].astype(F32) + adapter_scale_factor * difference).astype(BF)


def shards(
    activations,
    cotangent,
    resident_key_value_weight,
    down_master,
    down_first,
    down_second,
    up_master,
    up_first,
    up_second,
):
    tokens, features = activations.shape
    heads = cotangent.shape[1]
    shape = jax.ShapeDtypeStruct

    def exchange(value, axes):
        return lax.all_to_all(value, axes, 0, 0, tiled=True)

    own = kernel_call(
        spread_factors, shape((N_DP, SLOT, RANK), BF), 2, [pltpu.VMEM((SLOT, RANK), F32)]
    )(down_master, up_master)
    factors = exchange(own, ("yl", "z"))
    parts = kernel_call(
        project,
        shape((N_MP, tokens // N_MP, 2 * RANK), BF),
        3,
        [pltpu.VMEM((features, RANK), F32), pltpu.VMEM((heads, RANK), F32)],
    )(factors, activations, cotangent)
    parts = exchange(parts, "mp")
    total = kernel_call(add_parts, shape(parts.shape, BF), 1)(parts)
    full = exchange(total, "mp")
    grads = kernel_call(
        gradients,
        shape((N_DP, SLOT, RANK), BF),
        3,
        [
            pltpu.VMEM((features, RANK), F32),
            pltpu.VMEM((heads, RANK), F32),
            pltpu.VMEM((SLOT, RANK), F32),
        ],
    )(full, activations, cotangent)
    grads = exchange(grads, ("yl", "z"))
    state = (down_master, down_first, down_second, up_master, up_first, up_second)
    *new_state, send = kernel_call(
        update,
        [shape(a.shape, F32) for a in state] + [shape((N_YL * N_MP, SLOT, RANK), BF)],
        7,
        [pltpu.VMEM((SLOT, RANK), F32)],
    )(grads, *state)
    plane = exchange(send, ("yl", "mp"))
    place = jnp.stack([lax.axis_index("yl"), lax.axis_index("mp")]).astype(jnp.int32)
    routed = kernel_call(
        route, shape((N_Z, SLOT, RANK), BF), 2, [pltpu.VMEM((SLOT, RANK), F32)], smem=(0,)
    )(place, plane)
    arrived = exchange(routed, "z")
    merged = kernel_call(
        merge,
        shape(resident_key_value_weight.shape, BF),
        2,
        [pltpu.VMEM((N_Z * DOWN, RANK), F32), pltpu.VMEM((heads, RANK), F32)],
    )(arrived, resident_key_value_weight)
    return (merged, *new_state)


def solution(mesh):
    fine = Mesh(mesh.devices.reshape(N_YL, N_Z, N_MP), ("yl", "z", "mp"))
    dp = ("yl", "z")
    wide, state = P(dp, "mp"), P("mp", dp, None)
    return jax.shard_map(
        shards,
        mesh=fine,
        in_specs=(wide,) * 3 + (state,) * 6,
        out_specs=(wide,) + (state,) * 6,
        check_vma=False,
    )
```

time: 1560 us -> 161 us (0.10)
  the two profiles are of different devices: /device:TPU:1 before, /device:TPU:32 now
where the time goes in v1:
time: 161 us; the launch traced here: 160 us
  waiting for transfers between devices  74.9 us (47%)
  blocking collectives  39 us (24%)
  starting transfers between devices  28.7 us (18%)
  local copies, waits for them, and re-layouts  9.42 us (6%)
  Pallas kernels  6.86 us (4%)
    all_to_all x4, waiting for transfers between devices, exchange(): return lax.all_to_all(value, axes, 0, 0, tiled=True)  74.9 us
    all_to_all x2, blocking collectives, exchange(): return lax.all_to_all(value, axes, 0, 0, tiled=True)  39 us
    all_to_all x4, starting transfers between devices, exchange(): return lax.all_to_all(value, axes, 0, 0, tiled=True)  28.7 us
    unnamed x29, local copies, waits for them, and re-layouts  9.42 us
  transfers between devices with their start and end apart: 4, of which 4 were waited for; matrix products, arithmetic and copies ran while one was open for 3% of the time, Pallas kernels for 0%

profile of v1, /device:TPU:32, one launch (start us, length us, event | category | flops | bytes accessed | tf_op | source)
XLA Modules:
  0.0 159.8 jit_solution(5998712566304855182)
XLA Ops:
  0.6 0.7 copy.16.down_ref.dm_ref
  1.4 0.7 copy.17.up_ref.um_ref
  2.0 0.8 shard_map.144
  2.8 16.4 %all-to-all-start = ((bf16[32,48,128]{2,1,0:T(8,128)(2,1)}), bf16[32,48,128]{2,1,0:T(8,128)(2,1)S(1)}, u32[]{:S(2)}, u32[]{:S(2)}) async-start(bf16[32,48,128]{2,1,0:T(8,128)(2,1)} %shard_map.144), calls=%async_computation | async-start | bytes 786432 | tf_op jit(solution)/shard_map/all_to_all | solution.py:167
  19.2 1.3 copy.18.cot_ref
  20.5 25.2 %all-to-all-done.slots_ref = bf16[32,48,128]{2,1,0:T(8,128)(2,1)S(1)} async-done(((bf16[32,48,128]{2,1,0:T(8,128)(2,1)}), bf16[32,48,128]{2,1,0:T(8,128)(2,1)S(1)}, u32[]{:S(2)}, u32[]{:S(2)}) %all-to-all-start) | async-done | bytes 393248 | tf_op jit(solution)/shard_map/all_to_all | solution.py:167
  45.7 2.0 %copy-done = bf16[1536,1152]{1,0:T(8,128)(2,1)S(1)} copy-done((bf16[1536,1152]{1,0:T(8,128)(2,1)S(1)}, bf16[1536,1152]{1,0:T(8,128)(2,1)}, u32[]{:S(2)}) %copy-start) | copy-done | bytes 3538968
  47.7 1.3 shard_map.145
  49.0 0.0 copy-start.1
  49.0 21.6 %all_to_all.30.parts_ref = bf16[16,96,256]{2,1,0:T(8,128)(2,1)S(1)} all-to-all(bf16[16,96,256]{2,1,0:T(8,128)(2,1)S(1)} %shard_map.145), channel_id=1, replica_groups=mesh['yl'=2,'z'=16,'mp'=16] {'mp'}, dimensions={0} | all-to-all | bytes 1572864 | tf_op jit(solution)/shard_map/all_to_all | solution.py:167
  70.7 0.1 shard_map.146
  70.8 0.0 copy-start.3
  70.8 17.4 %all_to_all.31.full_ref = bf16[16,96,256]{2,1,0:T(8,128)(2,1)S(1)} all-to-all(bf16[16,96,256]{2,1,0:T(8,128)(2,1)S(1)} %shard_map.146), channel_id=1, replica_groups=mesh['yl'=2,'z'=16,'mp'=16] {'mp'}, dimensions={0} | all-to-all | bytes 1572864 | tf_op jit(solution)/shard_map/all_to_all | solution.py:167
  88.3 2.2 %shard_map.147 = bf16[32,48,128]{2,1,0:T(8,128)(2,1)} custom-call(bf16[16,96,256]{2,1,0:T(8,128)(2,1)S(1)} %all_to_all.31.full_ref, bf16[1536,1152]{1,0:T(8,128)(2,1)S(1)} %copy-done.1, bf16[1536,192]{1,0:T(8,128)(2,1)S(1)} %copy.18.cot_ref), custom_call_target="tpu_custom_call" | custom-call | tf_op jit(solution)/shard_map/pallas_call | solution.py:182
  90.5 4.4 %all-to-all-start.3 = ((bf16[32,48,128]{2,1,0:T(8,128)(2,1)}), bf16[32,48,128]{2,1,0:T(8,128)(2,1)S(1)}, u32[]{:S(2)}, u32[]{:S(2)}) async-start(bf16[32,48,128]{2,1,0:T(8,128)(2,1)} %shard_map.147), calls=%async_computation.3 | async-start | bytes 786432 | tf_op jit(solution)/shard_map/all_to_all | solution.py:167
  95.0 27.1 %all-to-all-done.3.parts_ref = bf16[32,48,128]{2,1,0:T(8,128)(2,1)S(1)} async-done(((bf16[32,48,128]{2,1,0:T(8,128)(2,1)}), bf16[32,48,128]{2,1,0:T(8,128)(2,1)S(1)}, u32[]{:S(2)}, u32[]{:S(2)}) %all-to-all-start.3) | async-done | bytes 393248 | tf_op jit(solution)/shard_map/all_to_all | solution.py:167
  122.1 0.9 shard_map.148
  122.9 3.9 %all-to-all-start.4 = ((bf16[32,48,128]{2,1,0:T(8,128)(2,1)}), bf16[32,48,128]{2,1,0:T(8,128)(2,1)S(1)}, u32[]{:S(2)}, u32[]{:S(2)}) async-start(bf16[32,48,128]{2,1,0:T(8,128)(2,1)} %get-tuple-element.14), calls=%async_computation.4 | async-start | bytes 786432 | tf_op jit(solution)/shard_map/all_to_all | solution.py:167
  126.8 0.1 pad_add_fusion.place_ref
  126.9 10.3 %all-to-all-done.4.plane_ref = bf16[32,48,128]{2,1,0:T(8,128)(2,1)S(1)} async-done(((bf16[32,48,128]{2,1,0:T(8,128)(2,1)}), bf16[32,48,128]{2,1,0:T(8,128)(2,1)S(1)}, u32[]{:S(2)}, u32[]{:S(2)}) %all-to-all-start.4) | async-done | bytes 393248 | tf_op jit(solution)/shard_map/all_to_all | solution.py:167
  137.1 1.3 shard_map.149
  138.5 4.1 %all-to-all-start.5 = ((bf16[16,48,128]{2,1,0:T(8,128)(2,1)}), bf16[16,48,128]{2,1,0:T(8,128)(2,1)S(1)}, u32[]{:S(2)}, u32[]{:S(2)}) async-start(bf16[16,48,128]{2,1,0:T(8,128)(2,1)} %shard_map.149), calls=%async_computation.5 | async-start | bytes 393216 | tf_op jit(solution)/shard_map/all_to_all | solution.py:167
  142.6 0.2 copy.26.base_ref
  142.7 0.6 copy.28
  143.4 0.6 copy.29
  144.0 0.6 copy.30
  144.6 0.6 copy.31
  145.2 0.6 copy.32
  145.8 0.6 copy.33
  146.4 12.3 %all-to-all-done.5.slots_ref = bf16[16,48,128]{2,1,0:T(8,128)(2,1)S(1)} async-done(((bf16[16,48,128]{2,1,0:T(8,128)(2,1)}), bf16[16,48,128]{2,1,0:T(8,128)(2,1)S(1)}, u32[]{:S(2)}, u32[]{:S(2)}) %all-to-all-start.5) | async-done | bytes 196640 | tf_op jit(solution)/shard_map/all_to_all | solution.py:167
  158.7 0.3 shard_map.150
  159.0 0.9 copy.27
  (15 shorter events, 0.0 us)
Async XLA Ops:
  2.8 42.9 %all-to-all-start = ((bf16[32,48,128]{2,1,0:T(8,128)(2,1)}), bf16[32,48,128]{2,1,0:T(8,128)(2,1)S(1)}, u32[]{:S(2)}, u32[]{:S(2)}) async-start(bf16[32,48,128]{2,1,0:T(8,128)(2,1)} %shard_map.144), calls=%async_computation | async-start | bytes 786432 | tf_op jit(solution)/shard_map/all_to_all | solution.py:167
  45.7 2.0 %copy-start = (bf16[1536,1152]{1,0:T(8,128)(2,1)S(1)}, bf16[1536,1152]{1,0:T(8,128)(2,1)}, u32[]{:S(2)}) copy-start(bf16[1536,1152]{1,0:T(8,128)(2,1)} %act_ref.3) | copy-start | bytes 10616836
  49.0 39.2 %copy-start.1 = (bf16[1536,1152]{1,0:T(8,128)(2,1)S(1)}, bf16[1536,1152]{1,0:T(8,128)(2,1)}, u32[]{:S(2)}) copy-start(bf16[1536,1152]{1,0:T(8,128)(2,1)} %act_ref.3) | copy-start | bytes 10616836
  70.8 24.1 %copy-start.3 = (f32[1,36,128]{2,0,1:T(1,128)S(1)}, f32[1,36,128]{2,0,1:T(1,128)}, u32[]{:S(2)}) copy-start(f32[1,36,128]{2,0,1:T(1,128)} %param.13) | copy-start | bytes 55300
  88.2 6.7 %copy-start.4 = (f32[1,36,128]{2,0,1:T(1,128)S(1)}, f32[1,36,128]{2,0,1:T(1,128)}, u32[]{:S(2)}) copy-start(f32[1,36,128]{2,0,1:T(1,128)} %param.14) | copy-start | bytes 55300
  88.2 6.7 %copy-start.5 = (f32[1,6,128]{2,0,1:T(1,128)S(1)}, f32[1,6,128]{2,0,1:T(1,128)}, u32[]{:S(2)}) copy-start(f32[1,6,128]{2,0,1:T(1,128)} %param.16) | copy-start | bytes 9220
  88.2 6.7 %copy-start.6 = (f32[1,6,128]{2,0,1:T(1,128)S(1)}, f32[1,6,128]{2,0,1:T(1,128)}, u32[]{:S(2)}) copy-start(f32[1,6,128]{2,0,1:T(1,128)} %param.17) | copy-start | bytes 9220
  88.2 54.3 %copy-start.2 = (bf16[576,192]{0,1:T(8,128)(2,1)S(1)}, bf16[576,192]{0,1:T(8,128)(2,1)}, u32[]{:S(2)}) copy-start(bf16[576,192]{0,1:T(8,128)(2,1)} %param.11) | copy-start | bytes 663556
  90.5 31.6 %all-to-all-start.3 = ((bf16[32,48,128]{2,1,0:T(8,128)(2,1)}), bf16[32,48,128]{2,1,0:T(8,128)(2,1)S(1)}, u32[]{:S(2)}, u32[]{:S(2)}) async-start(bf16[32,48,128]{2,1,0:T(8,128)(2,1)} %shard_map.147), calls=%async_computation.3 | async-start | bytes 786432 | tf_op jit(solution)/shard_map/all_to_all | solution.py:167
  122.9 14.2 %all-to-all-start.4 = ((bf16[32,48,128]{2,1,0:T(8,128)(2,1)}), bf16[32,48,128]{2,1,0:T(8,128)(2,1)S(1)}, u32[]{:S(2)}, u32[]{:S(2)}) async-start(bf16[32,48,128]{2,1,0:T(8,128)(2,1)} %get-tuple-element.14), calls=%async_computation.4 | async-start | bytes 786432 | tf_op jit(solution)/shard_map/all_to_all | solution.py:167
  138.5 20.2 %all-to-all-start.5 = ((bf16[16,48,128]{2,1,0:T(8,128)(2,1)}), bf16[16,48,128]{2,1,0:T(8,128)(2,1)S(1)}, u32[]{:S(2)}, u32[]{:S(2)}) async-start(bf16[16,48,128]{2,1,0:T(8,128)(2,1)} %shard_map.149), calls=%async_computation.5 | async-start | bytes 393216 | tf_op jit(solution)/shard_map/all_to_all | solution.py:167

commit v2 on v1

v2 whole, which is shorter than its diff:
```python
import jax
import jax.numpy as jnp
from jax import lax
from jax.experimental import pallas as pl
from jax.experimental.pallas import tpu as pltpu
from jax.sharding import Mesh
from jax.sharding import PartitionSpec as P

adapter_scale_factor = 2.0
learn_rate = 0.05
beta_one = 0.9
beta_two = 0.999
adam_eps = 1e-08
decay_rate = 0.01
step_count = 10.0

BF = jnp.bfloat16
F32 = jnp.float32
DOWN, UP, UP_AT, SLOT = 36, 6, 40, 48
N_YL, N_Z, N_MP = 2, 16, 16
N_DP = N_YL * N_Z
N_CORE = 2
N_ZQ, N_ZP = 8, 2
RANK = 128

VMEM = pl.BlockSpec(memory_space=pltpu.VMEM)
HBM = pl.BlockSpec(memory_space=pltpu.HBM)
SMEM = pl.BlockSpec(memory_space=pltpu.SMEM)


def adamw_update(master, first, second, grad):
    first_new = beta_one * first + (1.0 - beta_one) * grad
    second_new = beta_two * second + (1.0 - beta_two) * grad * grad
    first_hat = first_new / (1.0 - beta_one**step_count)
    second_hat = second_new / (1.0 - beta_two**step_count)
    master_new = master - learn_rate * (
        first_hat / (jnp.sqrt(second_hat) + adam_eps) + decay_rate * master
    )
    return (master_new, first_new, second_new)


def kernel_call(body, out_shape, n_in, scratch=(), smem=(), hbm=(), limit=32 * 2**20):
    many = isinstance(out_shape, (list, tuple))
    return pl.pallas_call(
        body,
        out_shape=out_shape,
        in_specs=[SMEM if i in smem else HBM if i in hbm else VMEM for i in range(n_in)],
        out_specs=[VMEM] * len(out_shape) if many else VMEM,
        scratch_shapes=list(scratch),
        compiler_params=pltpu.CompilerParams(vmem_limit_bytes=limit),
    )


def spread_factors(down_ref, up_ref, out_ref, slot):
    slot[...] = jnp.zeros_like(slot)
    slot[0:DOWN, :] = down_ref[:, 0, :]
    slot[UP_AT : UP_AT + UP, :] = up_ref[:, 0, :]
    value = slot[...].astype(BF)
    for j in range(out_ref.shape[0]):
        out_ref[j] = value


def unpack(slots_ref, factor, rows, at=0):
    for j in range(slots_ref.shape[0]):
        factor[j * rows : j * rows + rows, :] = slots_ref[j].astype(F32)[at : at + rows]


def fetch(act_in, cot_in, act_ref, cot_ref):
    act_ref[...] = act_in[...]
    cot_ref[...] = cot_in[...]


def project_half(half, a_use, bt_use, act_ref, cot_ref, out_ref):
    groups, rows, _ = out_ref.shape
    tokens = groups * rows
    first = pl.multiple_of(half * tokens, tokens)
    back = lax.dot_general(
        cot_ref[:, pl.ds(first, tokens)],
        bt_use,
        (((0,), (0,)), ((), ())),
        preferred_element_type=F32,
    )
    out_ref[:, :, RANK:] = back.astype(BF).reshape(groups, rows, RANK)
    step = groups // 2
    for i in range(0, groups, step):
        at = pl.ds(pl.multiple_of(first + i * rows, step * rows), step * rows)
        hidden = jnp.dot(act_ref[at, :], a_use, preferred_element_type=F32)
        out_ref[i : i + step, :, 0:RANK] = hidden.astype(BF).reshape(step, rows, RANK)


def project_other(place_ref, slots_ref, act_ref, cot_ref, out_ref, a_ref, bt_ref, down, up):
    unpack(slots_ref, down, DOWN)
    unpack(slots_ref, up, UP, UP_AT)
    a_ref[...] = down[...].astype(BF)
    bt_ref[...] = up[...].astype(BF)
    project_half(1 - place_ref[0], a_ref[...], bt_ref[...], act_ref, cot_ref, out_ref)


def project_own(place_ref, a_ref, bt_ref, act_ref, cot_ref, out_ref):
    project_half(place_ref[0], a_ref[...], bt_ref[...], act_ref, cot_ref, out_ref)


def sum_parts(parts_ref):
    total = parts_ref[0].astype(F32)
    for j in range(1, parts_ref.shape[0]):
        total += parts_ref[j].astype(F32)
    return total


def add_parts(parts_ref, out_ref):
    value = sum_parts(parts_ref).astype(BF)
    for j in range(out_ref.shape[0]):
        out_ref[j] = value


def add_pair(one_ref, two_ref, out_ref):
    out_ref[...] = (one_ref[...].astype(F32) + two_ref[...].astype(F32)).astype(BF)


def gradients(full_ref, act_ref, cot_ref, out_ref, down, up, slot):
    tokens = act_ref.shape[0]
    full = full_ref[...].reshape(tokens, 2 * RANK)
    hidden, back = full[:, 0:RANK], full[:, RANK:]
    down[...] = adapter_scale_factor * lax.dot_general(
        act_ref[...], back, (((0,), (0,)), ((), ())), preferred_element_type=F32
    )
    up[...] = adapter_scale_factor * jnp.dot(
        cot_ref[...], hidden, preferred_element_type=F32
    )
    for near in range(N_YL * N_ZP):
        y_lo, zp = divmod(near, N_ZP)
        for zq in range(N_ZQ):
            j = y_lo * N_Z + zq * N_ZP + zp
            at = zq * (DOWN + UP)
            slot[at : at + DOWN, :] = down[j * DOWN : j * DOWN + DOWN, :]
            slot[at + DOWN : at + DOWN + UP, :] = up[j * UP : j * UP + UP, :]
        out_ref[near] = slot[...].astype(BF)


def add_near(parts_ref, out_ref, total, slot):
    total[...] = sum_parts(parts_ref)
    slot[...] = jnp.zeros_like(slot)
    for zq in range(N_ZQ):
        at = zq * (DOWN + UP)
        slot[0:DOWN, :] = total[at : at + DOWN, :]
        slot[UP_AT : UP_AT + UP, :] = total[at + DOWN : at + DOWN + UP, :]
        out_ref[zq] = slot[...].astype(BF)


def update(
    parts_ref, dm_ref, df_ref, ds_ref, um_ref, uf_ref, us_ref,
    dm_out, df_out, ds_out, um_out, uf_out, us_out, down_send, up_send, slot,
):
    total = sum_parts(parts_ref)
    down_new = adamw_update(
        dm_ref[:, 0, :], df_ref[:, 0, :], ds_ref[:, 0, :], total[0:DOWN]
    )
    up_new = adamw_update(
        um_ref[:, 0, :], uf_ref[:, 0, :], us_ref[:, 0, :], total[UP_AT : UP_AT + UP]
    )
    dm_out[:, 0, :], df_out[:, 0, :], ds_out[:, 0, :] = down_new
    um_out[:, 0, :], uf_out[:, 0, :], us_out[:, 0, :] = up_new
    slot[...] = jnp.zeros_like(slot)
    slot[0:DOWN, :] = down_new[0]
    slot[UP_AT : UP_AT + UP, :] = up_new[0]
    down_send[...] = slot[0:UP_AT, :].astype(BF)
    value = slot[UP_AT:SLOT, :].astype(BF)
    for j in range(N_DP):
        up_send[j] = value


def merge(down_ref, up_ref, base_ref, out_ref, down, up):
    unpack(down_ref, down, DOWN)
    unpack(up_ref, up, UP)
    difference = lax.dot_general(
        up[...].astype(BF),
        down[...].astype(BF),
        (((1,), (1,)), ((), ())),
        preferred_element_type=F32,
    )
    out_ref[...] = (base_ref[...].astype(F32) + adapter_scale_factor * difference).astype(BF)


def spread_rows(rows_ref, out_ref):
    value = rows_ref[...]
    for j in range(out_ref.shape[0]):
        out_ref[j] = value


def owner_to_base(i):
    dp, mp = divmod(i, N_MP)
    y_lo, z = divmod(dp, N_Z)
    return (2 * mp + y_lo) * N_MP + z


def shards(
    activations,
    cotangent,
    resident_key_value_weight,
    down_master,
    down_first,
    down_second,
    up_master,
    up_first,
    up_second,
):
    tokens, features = activations.shape
    heads = cotangent.shape[1]
    shape = jax.ShapeDtypeStruct
    dp, mp = ("yl", "zq", "zp"), ("xy", "core")
    cotangent_t = cotangent.T
    base_t = resident_key_value_weight.T
    state = [a.reshape(DOWN, 1, RANK) for a in (down_master, down_first, down_second)]
    state += [a.reshape(UP, 1, RANK) for a in (up_master, up_first, up_second)]

    def exchange(value, axes):
        return lax.all_to_all(value, axes, 0, 0, tiled=True)

    def wide(rows):
        return pltpu.VMEM((rows, RANK), F32)

    activations, cotangent_t = kernel_call(
        fetch,
        [shape(activations.shape, BF), shape(cotangent_t.shape, BF)],
        2,
        limit=32 * 2**20,
    )(activations, cotangent_t)
    own = kernel_call(spread_factors, shape((N_Z, SLOT, RANK), BF), 2, [wide(SLOT)])(
        state[0], state[3]
    )
    factors = lax.all_gather(exchange(own, ("zq", "zp")), "yl", axis=0, tiled=True)
    core = lax.axis_index("core").astype(jnp.int32).reshape(1)
    half = shape((N_MP // N_CORE, tokens // N_MP, 2 * RANK), BF)
    other_half, a_use, bt_use = kernel_call(
        project_other,
        [half, shape((features, RANK), BF), shape((heads, RANK), BF)],
        4,
        [wide(features), wide(heads)],
        smem=(0,),
    )(core, factors, activations, cotangent_t)
    other_half = lax.ppermute(other_half, "core", [(0, 1), (1, 0)])
    own_half = kernel_call(project_own, half, 5, smem=(0,))(
        core, a_use, bt_use, activations, cotangent_t
    )
    own_half = kernel_call(add_pair, half, 2)(own_half, other_half)
    own_half = exchange(own_half, "xy")
    own_half = exchange(kernel_call(add_parts, half, 1)(own_half), "xy")
    full = lax.all_gather(own_half, "core", axis=0, tiled=True)
    near_rows = N_ZQ * (DOWN + UP)
    grads = kernel_call(
        gradients,
        shape((N_YL * N_ZP, near_rows, RANK), BF),
        3,
        [wide(features), wide(heads), wide(near_rows)],
    )(full, activations, cotangent_t)
    grads = exchange(grads, ("yl", "zp"))
    grads = kernel_call(
        add_near, shape((N_ZQ, SLOT, RANK), BF), 1, [wide(near_rows), wide(SLOT)]
    )(grads)
    grads = exchange(grads, "zq")
    *new, down_send, up_send = kernel_call(
        update,
        [shape(a.shape, F32) for a in state]
        + [shape((UP_AT, RANK), BF), shape((N_DP, SLOT - UP_AT, RANK), BF)],
        7,
        [wide(SLOT)],
    )(grads, *state)
    devices = N_DP * N_MP
    down_piece = lax.ppermute(
        down_send, dp + mp, [(i, owner_to_base(i)) for i in range(devices)]
    )
    up_rows = exchange(up_send, dp)
    down_piece, up_rows = lax.optimization_barrier((down_piece, up_rows))
    pieces = kernel_call(spread_rows, shape((N_MP, UP_AT, RANK), BF), 1)(down_piece)
    down_rows = exchange(pieces, mp)
    merged = kernel_call(
        merge, shape(base_t.shape, BF), 3, [wide(N_Z * DOWN), wide(heads)]
    )(down_rows, up_rows, base_t)
    return (merged.T, *[a.reshape(1, a.shape[0], RANK) for a in new])


def solution(mesh):
    sizes = (N_YL, N_ZQ, N_ZP, N_MP // N_CORE, N_CORE)
    fine = Mesh(mesh.devices.reshape(sizes), ("yl", "zq", "zp", "xy", "core"))
    dp, mp = ("yl", "zq", "zp"), ("xy", "core")
    wide, state = P(dp, mp), P(mp, dp, None)
    return jax.shard_map(
        shards,
        mesh=fine,
        in_specs=(wide,) * 3 + (state,) * 6,
        out_specs=(wide,) + (state,) * 6,
        check_vma=False,
    )
```

time: 161 us -> 146 us (0.907)
  the two profiles are of different devices: /device:TPU:32 before, /device:TPU:1 now
where the time goes in v2:
time: 146 us; the launch traced here: 145 us
  blocking collectives  80.6 us (55%)
  starting transfers between devices  34.9 us (24%)
  waiting for transfers between devices  15.2 us (10%)
  local copies, waits for them, and re-layouts  7.32 us (5%)
  Pallas kernels  5.96 us (4%)
    all_to_all x5, blocking collectives, exchange(): return lax.all_to_all(value, axes, 0, 0, tiled=True)  70.3 us
    all_to_all x2, starting transfers between devices, exchange(): return lax.all_to_all(value, axes, 0, 0, tiled=True)  20.1 us
    all_to_all x2, waiting for transfers between devices, exchange(): return lax.all_to_all(value, axes, 0, 0, tiled=True)  13.9 us
    ppermute x1, starting transfers between devices, shards(): other_half = lax.ppermute(other_half, 'core', [(0, 1), (1, 0)])  7.9 us
    unnamed x28, local copies, waits for them, and re-layouts  7.32 us
    ppermute x1, starting transfers between devices, shards(): lax.ppermute(down_send, dp + mp, [(i, owner_to_base(i)) for i in range(de...  6.97 us
    all_gather x1, blocking collectives, shards(): lax.all_gather(exchange(own, ('zq', 'zp')), 'yl', axis=0, tiled=True)  5.4 us
    all_gather x1, blocking collectives, shards(): full = lax.all_gather(own_half, 'core', axis=0, tiled=True)  4.9 us
  transfers between devices with their start and end apart: 4, of which 4 were waited for; matrix products, arithmetic and copies ran while one was open for 0% of the time, Pallas kernels for 1%

profile of v2, /device:TPU:1, one launch (start us, length us, event | category | flops | bytes accessed | tf_op | source)
XLA Modules:
  0.0 144.8 jit_solution(5479993394700317107)
XLA Ops:
  0.6 0.7 copy-done.6
  1.4 0.7 copy-done.10
  2.0 0.7 shard_map.144
  2.7 15.8 %all-to-all-start = ((bf16[16,48,128]{2,1,0:T(8,128)(2,1)}), bf16[16,48,128]{2,1,0:T(8,128)(2,1)}, u32[]{:S(2)}, u32[]{:S(2)}) async-start(bf16[16,48,128]{2,1,0:T(8,128)(2,1)} %shard_map.144), calls=%async_computation | async-start | bytes 393216 | tf_op jit(solution)/shard_map/all_to_all | solution.py:217
  18.6 2.0 %copy-done.3 = bf16[1536,1152]{1,0:T(8,128)(2,1)S(1)} copy-done((bf16[1536,1152]{1,0:T(8,128)(2,1)S(1)}, bf16[1536,1152]{1,0:T(8,128)(2,1)}, u32[]{:S(2)}) %copy-start.3) | copy-done | bytes 3538968
  20.6 1.1 copy-done.4
  21.6 0.3 shard_map.145
  21.9 0.8 copy-done
  22.7 8.4 %all-to-all-done = bf16[16,48,128]{2,1,0:T(8,128)(2,1)} async-done(((bf16[16,48,128]{2,1,0:T(8,128)(2,1)}), bf16[16,48,128]{2,1,0:T(8,128)(2,1)}, u32[]{:S(2)}, u32[]{:S(2)}) %all-to-all-start) | async-done | bytes 196640 | tf_op jit(solution)/shard_map/all_to_all | solution.py:217
  31.2 5.4 %all_gather.6.slots_ref = bf16[32,48,128]{2,1,0:T(8,128)(2,1)S(1)} all-gather(bf16[16,48,128]{2,1,0:T(8,128)(2,1)} %all-to-all-done), channel_id=1, replica_groups=mesh['yl'=2,'zq'=8,'zp'=2,'xy'=8,'core'=2] {'yl'}, dimensions={0}, use_global_device_ids=true | all-gather | bytes 589824 | tf_op jit(solution)/shard_map/all_gather | solution.py:231
  36.6 1.1 copy-done.1
  37.6 0.8 shard_map.146
  38.5 7.9 %collective-permute-start = (bf16[8,96,256]{2,1,0:T(8,128)(2,1)S(1)}, bf16[8,96,256]{2,1,0:T(8,128)(2,1)S(1)}, u32[]{:S(2)}, u32[]{:S(2)}) collective-permute-start(bf16[8,96,256]{2,1,0:T(8,128)(2,1)S(1)} %get-tuple-element.26), channel_id=1, source_target_pairs={{0,1},{1,0},{2,3},{3,2},{4,5},{5,4},{6,7},{7,6},{8,9},{9,8},{10,11... | collective-permute-start | bytes 1179656 | tf_op jit(solution)/shard_map/ppermute | solution.py:241
  46.4 0.8 shard_map.147.one_ref
  47.1 0.5 collective-permute-done.two_ref
  47.7 0.1 shard_map.148
  47.8 15.2 %all_to_all.35.parts_ref = bf16[8,96,256]{2,1,0:T(8,128)(2,1)S(1)} all-to-all(bf16[8,96,256]{2,1,0:T(8,128)(2,1)S(1)} %shard_map.148), channel_id=1, replica_groups=mesh['yl'=2,'zq'=8,'zp'=2,'xy'=8,'core'=2] {'xy'}, dimensions={0} | all-to-all | bytes 786432 | tf_op jit(solution)/shard_map/all_to_all | solution.py:217
  63.0 0.1 shard_map.149
  63.1 11.4 %all_to_all.36 = bf16[8,96,256]{2,1,0:T(8,128)(2,1)S(1)} all-to-all(bf16[8,96,256]{2,1,0:T(8,128)(2,1)S(1)} %shard_map.149), channel_id=1, replica_groups=mesh['yl'=2,'zq'=8,'zp'=2,'xy'=8,'core'=2] {'xy'}, dimensions={0} | all-to-all | bytes 786432 | tf_op jit(solution)/shard_map/all_to_all | solution.py:217
  74.5 4.9 %all_gather.7.full_ref = bf16[16,96,256]{2,1,0:T(8,128)(2,1)S(1)} all-gather(bf16[8,96,256]{2,1,0:T(8,128)(2,1)S(1)} %all_to_all.36), channel_id=1, replica_groups=mesh['yl'=2,'zq'=8,'zp'=2,'xy'=8,'core'=2] {'core'}, dimensions={0}, use_global_device_ids=true | all-gather | bytes 1179648 | tf_op jit(solution)/shard_map/all_gather | solution.py:248
  79.4 1.4 shard_map.150
  80.8 8.3 %all_to_all.37.parts_ref = bf16[4,336,128]{2,1,0:T(8,128)(2,1)S(1)} all-to-all(bf16[4,336,128]{2,1,0:T(8,128)(2,1)S(1)} %shard_map.150), channel_id=1, replica_groups=mesh['yl'=2,'zq'=8,'zp'=2,'xy'=8,'core'=2] {'yl','zp'}, dimensions={0} | all-to-all | bytes 688128 | tf_op jit(solution)/shard_map/all_to_all | solution.py:217
  89.2 0.1 shard_map.151
  89.3 17.7 %all_to_all.38.parts_ref = bf16[8,48,128]{2,1,0:T(8,128)(2,1)S(1)} all-to-all(bf16[8,48,128]{2,1,0:T(8,128)(2,1)S(1)} %shard_map.151), channel_id=1, replica_groups=mesh['yl'=2,'zq'=8,'zp'=2,'xy'=8,'core'=2] {'zq'}, dimensions={0} | all-to-all | bytes 196608 | tf_op jit(solution)/shard_map/all_to_all | solution.py:217
  107.0 0.8 shard_map.152
  107.8 4.3 %all-to-all-start.5 = ((bf16[32,8,128]{2,1,0:T(8,128)(2,1)}), bf16[32,8,128]{2,1,0:T(8,128)(2,1)S(1)}, u32[]{:S(2)}, u32[]{:S(2)}) async-start(bf16[32,8,128]{2,1,0:T(8,128)(2,1)} %get-tuple-element.28), calls=%async_computation.5 | async-start | bytes 131072 | tf_op jit(solution)/shard_map/all_to_all | solution.py:217
  112.1 7.0 %collective-permute-start.1 = (bf16[40,128]{1,0:T(8,128)(2,1)S(1)}, bf16[40,128]{1,0:T(8,128)(2,1)S(1)}, u32[]{:S(2)}, u32[]{:S(2)}) collective-permute-start(bf16[40,128]{1,0:T(8,128)(2,1)S(1)} %get-tuple-element.27), channel_id=1, source_target_pairs={{0,0},{1,32},{2,64},{3,96},{4,128},{5,160},{6,192},{7,224},{8,256}... | collective-permute-start | bytes 30728 | tf_op jit(solution)/shard_map/ppermute | solution.py:269
  119.1 0.8 collective-permute-done.1.rows_ref
  119.9 5.4 %all-to-all-done.5.up_ref = bf16[32,8,128]{2,1,0:T(8,128)(2,1)S(1)} async-done(((bf16[32,8,128]{2,1,0:T(8,128)(2,1)}), bf16[32,8,128]{2,1,0:T(8,128)(2,1)S(1)}, u32[]{:S(2)}, u32[]{:S(2)}) %all-to-all-start.5) | async-done | bytes 65568 | tf_op jit(solution)/shard_map/all_to_all | solution.py:217
  125.4 17.6 %all_to_all.39.down_ref = bf16[16,40,128]{2,1,0:T(8,128)(2,1)S(1)} all-to-all(bf16[16,40,128]{2,1,0:T(8,128)(2,1)S(1)} %shard_map.153), channel_id=1, replica_groups=mesh['yl'=2,'zq'=8,'zp'=2,'xy'=8,'core'=2] {'xy','core'}, dimensions={0} | all-to-all | bytes 327680 | tf_op jit(solution)/shard_map/all_to_all | solution.py:217
  142.9 0.9 copy-done.5
  143.9 0.9 shard_map.154
  (22 shorter events, 0.1 us)
Async XLA Ops:
  0.6 0.7 copy-start.6
  1.4 0.7 copy-start.10
  2.7 28.4 %all-to-all-start = ((bf16[16,48,128]{2,1,0:T(8,128)(2,1)}), bf16[16,48,128]{2,1,0:T(8,128)(2,1)}, u32[]{:S(2)}, u32[]{:S(2)}) async-start(bf16[16,48,128]{2,1,0:T(8,128)(2,1)} %shard_map.144), calls=%async_computation | async-start | bytes 393216 | tf_op jit(solution)/shard_map/all_to_all | solution.py:217
  18.5 2.0 %copy-start.3 = (bf16[1536,1152]{1,0:T(8,128)(2,1)S(1)}, bf16[1536,1152]{1,0:T(8,128)(2,1)}, u32[]{:S(2)}) copy-start(bf16[1536,1152]{1,0:T(8,128)(2,1)} %act_in.1) | copy-start | bytes 10616836
  20.6 1.1 copy-start.4
  21.9 0.8 copy-start
  36.6 1.1 copy-start.1
  38.5 9.2 %collective-permute-start = (bf16[8,96,256]{2,1,0:T(8,128)(2,1)S(1)}, bf16[8,96,256]{2,1,0:T(8,128)(2,1)S(1)}, u32[]{:S(2)}, u32[]{:S(2)}) collective-permute-start(bf16[8,96,256]{2,1,0:T(8,128)(2,1)S(1)} %get-tuple-element.26), channel_id=1, source_target_pairs={{0,1},{1,0},{2,3},{3,2},{4,5},{5,4},{6,7},{7,6},{8,9},{9,8},{10,11... | collective-permute-start | bytes 1179656 | tf_op jit(solution)/shard_map/ppermute | solution.py:241
  47.1 32.3 %copy-start.2 = (bf16[192,1536]{1,0:T(8,128)(2,1)S(1)}, bf16[192,1536]{1,0:T(8,128)(2,1)}, u32[]{:S(2)}) copy-start(bf16[192,1536]{1,0:T(8,128)(2,1)} %copy-done) | copy-start | bytes 1769476
  79.4 27.6 %copy-start.7 = (f32[1,36,128]{2,0,1:T(1,128)S(1)}, f32[1,36,128]{2,0,1:T(1,128)}, u32[]{:S(2)}) copy-start(f32[1,36,128]{2,0,1:T(1,128)} %param.12) | copy-start | bytes 55300
  79.4 27.6 %copy-start.8 = (f32[1,36,128]{2,0,1:T(1,128)S(1)}, f32[1,36,128]{2,0,1:T(1,128)}, u32[]{:S(2)}) copy-start(f32[1,36,128]{2,0,1:T(1,128)} %param.13) | copy-start | bytes 55300
  79.4 27.6 %copy-start.9 = (f32[1,36,128]{2,0,1:T(1,128)S(1)}, f32[1,36,128]{2,0,1:T(1,128)}, u32[]{:S(2)}) copy-start(f32[1,36,128]{2,0,1:T(1,128)} %param.14) | copy-start | bytes 55300
  79.4 27.6 %copy-start.11 = (f32[1,6,128]{2,0,1:T(1,128)S(1)}, f32[1,6,128]{2,0,1:T(1,128)}, u32[]{:S(2)}) copy-start(f32[1,6,128]{2,0,1:T(1,128)} %param.15) | copy-start | bytes 9220
  79.4 27.6 %copy-start.12 = (f32[1,6,128]{2,0,1:T(1,128)S(1)}, f32[1,6,128]{2,0,1:T(1,128)}, u32[]{:S(2)}) copy-start(f32[1,6,128]{2,0,1:T(1,128)} %param.16) | copy-start | bytes 9220
  79.4 27.6 %copy-start.13 = (f32[1,6,128]{2,0,1:T(1,128)S(1)}, f32[1,6,128]{2,0,1:T(1,128)}, u32[]{:S(2)}) copy-start(f32[1,6,128]{2,0,1:T(1,128)} %param.17) | copy-start | bytes 9220
  107.8 17.5 %all-to-all-start.5 = ((bf16[32,8,128]{2,1,0:T(8,128)(2,1)}), bf16[32,8,128]{2,1,0:T(8,128)(2,1)S(1)}, u32[]{:S(2)}, u32[]{:S(2)}) async-start(bf16[32,8,128]{2,1,0:T(8,128)(2,1)} %get-tuple-element.28), calls=%async_computation.5 | async-start | bytes 131072 | tf_op jit(solution)/shard_map/all_to_all | solution.py:217
  112.1 7.8 %collective-permute-start.1 = (bf16[40,128]{1,0:T(8,128)(2,1)S(1)}, bf16[40,128]{1,0:T(8,128)(2,1)S(1)}, u32[]{:S(2)}, u32[]{:S(2)}) collective-permute-start(bf16[40,128]{1,0:T(8,128)(2,1)S(1)} %get-tuple-element.27), channel_id=1, source_target_pairs={{0,0},{1,32},{2,64},{3,96},{4,128},{5,160},{6,192},{7,224},{8,256}... | collective-permute-start | bytes 30728 | tf_op jit(solution)/shard_map/ppermute | solution.py:269
  142.9 0.9 copy-start.5

commit v3 on v2

--- a/solution.py
+++ b/solution.py
@@ -88,16 +88,20 @@
         out_ref[i : i + step, :, 0:RANK] = hidden.astype(BF).reshape(step, rows, RANK)
 
 
-def project_other(place_ref, slots_ref, act_ref, cot_ref, out_ref, a_ref, bt_ref, down, up):
-    unpack(slots_ref, down, DOWN)
-    unpack(slots_ref, up, UP, UP_AT)
+def project_other(slots_ref, slots_other_ref, act_ref, cot_ref, out_ref, a_ref, bt_ref, down, up):
+    low = lax.axis_index("yl") == 0
+    for z in range(N_Z):
+        own, other = slots_ref[z].astype(F32), slots_other_ref[z].astype(F32)
+        for j, value in ((z, jnp.where(low, own, other)), (N_Z + z, jnp.where(low, other, own))):
+            down[j * DOWN : j * DOWN + DOWN, :] = value[0:DOWN]
+            up[j * UP : j * UP + UP, :] = value[UP_AT : UP_AT + UP]
     a_ref[...] = down[...].astype(BF)
     bt_ref[...] = up[...].astype(BF)
-    project_half(1 - place_ref[0], a_ref[...], bt_ref[...], act_ref, cot_ref, out_ref)
-
-
-def project_own(place_ref, a_ref, bt_ref, act_ref, cot_ref, out_ref):
-    project_half(place_ref[0], a_ref[...], bt_ref[...], act_ref, cot_ref, out_ref)
+    project_half(1 - lax.axis_index("core"), a_ref[...], bt_ref[...], act_ref, cot_ref, out_ref)
+
+
+def project_own(a_ref, bt_ref, act_ref, cot_ref, out_ref):
+    project_half(lax.axis_index("core"), a_ref[...], bt_ref[...], act_ref, cot_ref, out_ref)
 
 
 def sum_parts(parts_ref):
@@ -170,7 +174,9 @@
 
 
 def merge(down_ref, up_ref, base_ref, out_ref, down, up):
-    unpack(down_ref, down, DOWN)
+    block = lax.axis_index("yl") * N_Z + lax.axis_index("zq") * N_ZP + lax.axis_index("zp")
+    for z in range(N_Z):
+        down[z * DOWN : z * DOWN + DOWN, :] = down_ref[base_slot(block, z)].astype(F32)[0:DOWN]
     unpack(up_ref, up, UP)
     difference = lax.dot_general(
         up[...].astype(BF),
@@ -181,16 +187,36 @@
     out_ref[...] = (base_ref[...].astype(F32) + adapter_scale_factor * difference).astype(BF)
 
 
+def hold(value_ref, out_ref):
+    out_ref[...] = value_ref[...]
+
+
 def spread_rows(rows_ref, out_ref):
     value = rows_ref[...]
     for j in range(out_ref.shape[0]):
         out_ref[j] = value
 
 
+NEAR_X = sum(v << 2 * i for i, v in enumerate((0, 1, 3, 0, 2, 1, 3, 2)))
+NEAR_Y = sum(v << 2 * i for i, v in enumerate((0, 0, 0, 1, 0, 1, 1, 1)))
+
+
+def base_slot(block, z):
+    turn = (z - block % N_Z + 2 * N_Z - 1) % N_Z - (N_Z // 2 - 1)
+    farther, nearer = -2 * turn, 2 * turn - 1
+    rank = max(farther, nearer) if isinstance(turn, int) else jnp.maximum(farther, nearer)
+    place = 2 * (rank // 2)
+    owner = block // 2
+    x = (owner // 4 + ((NEAR_X >> place) & 3)) % 4
+    y = (owner // 2 + ((NEAR_Y >> place) & 3)) % 2
+    return x * 4 + y * 2 + rank % 2
+
+
 def owner_to_base(i):
     dp, mp = divmod(i, N_MP)
     y_lo, z = divmod(dp, N_Z)
-    return (2 * mp + y_lo) * N_MP + z
+    block = 2 * mp + y_lo
+    return block * N_MP + base_slot(block, z)
 
 
 def shards(
@@ -228,19 +254,18 @@
     own = kernel_call(spread_factors, shape((N_Z, SLOT, RANK), BF), 2, [wide(SLOT)])(
         state[0], state[3]
     )
-    factors = lax.all_gather(exchange(own, ("zq", "zp")), "yl", axis=0, tiled=True)
-    core = lax.axis_index("core").astype(jnp.int32).reshape(1)
+    factors = exchange(own, ("zq", "zp"))
+    factors_other = lax.ppermute(factors, "yl", [(0, 1), (1, 0)])
     half = shape((N_MP // N_CORE, tokens // N_MP, 2 * RANK), BF)
     other_half, a_use, bt_use = kernel_call(
         project_other,
         [half, shape((features, RANK), BF), shape((heads, RANK), BF)],
         4,
         [wide(features), wide(heads)],
-        smem=(0,),
-    )(core, factors, activations, cotangent_t)
+    )(factors, factors_other, activations, cotangent_t)
     other_half = lax.ppermute(other_half, "core", [(0, 1), (1, 0)])
-    own_half = kernel_call(project_own, half, 5, smem=(0,))(
-        core, a_use, bt_use, activations, cotangent_t
+    own_half = kernel_call(project_own, half, 4)(
+        a_use, bt_use, activations, cotangent_t
     )
     own_half = kernel_call(add_pair, half, 2)(own_half, other_half)
     own_half = exchange(own_half, "xy")
@@ -265,13 +290,15 @@
         7,
         [wide(SLOT)],
     )(grads, *state)
+    base_t, up_send = lax.optimization_barrier((base_t, up_send))
+    base_t = kernel_call(hold, shape(base_t.shape, BF), 1)(base_t)
     devices = N_DP * N_MP
     down_piece = lax.ppermute(
         down_send, dp + mp, [(i, owner_to_base(i)) for i in range(devices)]
     )
     up_rows = exchange(up_send, dp)
-    down_piece, up_rows = lax.optimization_barrier((down_piece, up_rows))
     pieces = kernel_call(spread_rows, shape((N_MP, UP_AT, RANK), BF), 1)(down_piece)
+    pieces, up_rows, base_t = lax.optimization_barrier((pieces, up_rows, base_t))
     down_rows = exchange(pieces, mp)
     merged = kernel_call(
         merge, shape(base_t.shape, BF), 3, [wide(N_Z * DOWN), wide(heads)]

time: 146 us -> 141 us (0.966)
  blocking collectives: 80.6 us -> 97.6 us
  starting transfers between devices: 34.9 us -> 19.2 us
  local copies, waits for them, and re-layouts: 7.32 us -> 4.49 us
  waiting for transfers between devices: 15.2 us -> 12.5 us
    all_to_all x5 -> x6, blocking collectives: 70.3 us -> 92.7 us  [exchange(): return lax.all_to_all(value, axes, 0, 0, tiled=True)]
    all_to_all x2 -> x1, starting transfers between devices: 20.1 us -> 4.26 us  [exchange(): return lax.all_to_all(value, axes, 0, 0, tiled=True)]
    all_to_all x2 -> x1, waiting for transfers between devices: 13.9 us -> 0.01 us  [exchange(): return lax.all_to_all(value, axes, 0, 0, tiled=True)]
    ppermute x1, waiting for transfers between devices: 0.79 us -> 11.9 us  [shards(): lax.ppermute(down_send, dp + mp, [(i, owner_to_base(i)) for i in range(de...]
    all_gather x1 -> x0, blocking collectives: 5.4 us -> none  [shards(): lax.all_gather(exchange(own, ('zq', 'zp')), 'yl', axis=0, tiled=True)]
    ppermute x0 -> x1, starting transfers between devices: none -> 3.19 us  [shards(): factors_other = lax.ppermute(factors, 'yl', [(0, 1), (1, 0)])]
    ppermute x1, starting transfers between devices: 6.97 us -> 4 us  [shards(): lax.ppermute(down_send, dp + mp, [(i, owner_to_base(i)) for i in range(de...]
    unnamed x28 -> x22, local copies, waits for them, and re-layouts: 7.32 us -> 4.49 us
  transfers between devices with their start and end apart: 4 -> 4, of which waited for: 4 -> 2; matrix products, arithmetic and copies ran while one was open for 0% -> 0% of each run, Pallas kernels for 1% -> 1%
where the time goes in v3:
time: 141 us; the launch traced here: 140 us
  blocking collectives  97.6 us (69%)
  starting transfers between devices  19.2 us (14%)
  waiting for transfers between devices  12.5 us (9%)
  Pallas kernels  5.48 us (4%)
  local copies, waits for them, and re-layouts  4.49 us (3%)
    all_to_all x6, blocking collectives, exchange(): return lax.all_to_all(value, axes, 0, 0, tiled=True)  92.7 us
    ppermute x1, waiting for transfers between devices, shards(): lax.ppermute(down_send, dp + mp, [(i, owner_to_base(i)) for i in range(de...  11.9 us
    ppermute x1, starting transfers between devices, shards(): other_half = lax.ppermute(other_half, 'core', [(0, 1), (1, 0)])  7.71 us
    all_gather x1, blocking collectives, shards(): full = lax.all_gather(own_half, 'core', axis=0, tiled=True)  4.9 us
    unnamed x22, local copies, waits for them, and re-layouts  4.49 us
    all_to_all x1, starting transfers between devices, exchange(): return lax.all_to_all(value, axes, 0, 0, tiled=True)  4.26 us
    ppermute x1, starting transfers between devices, shards(): lax.ppermute(down_send, dp + mp, [(i, owner_to_base(i)) for i in range(de...  4 us
    ppermute x1, starting transfers between devices, shards(): factors_other = lax.ppermute(factors, 'yl', [(0, 1), (1, 0)])  3.19 us
  transfers between devices with their start and end apart: 4, of which 2 were waited for; matrix products, arithmetic and copies ran while one was open for 0% of the time, Pallas kernels for 1%

profile of v3, /device:TPU:1, one launch (start us, length us, event | category | flops | bytes accessed | tf_op | source)
XLA Modules:
  0.0 140.0 jit_solution(12083791658853587378)
XLA Ops:
  0.6 0.0 copy-start.3
  0.6 0.7 copy-done.3
  1.4 0.7 copy-done.7
  2.1 28.1 %all_to_all.35.slots_ref = bf16[16,48,128]{2,1,0:T(8,128)(2,1)S(1)} all-to-all(bf16[16,48,128]{2,1,0:T(8,128)(2,1)S(1)} %shard_map.144), channel_id=1, replica_groups=mesh['yl'=2,'zq'=8,'zp'=2,'xy'=8,'core'=2] {'zq','zp'}, dimensions={0} | all-to-all | bytes 393216 | tf_op jit(solution)/shard_map/all_to_all | solution.py:243
  30.2 3.2 %collective-permute-start = (bf16[16,48,128]{2,1,0:T(8,128)(2,1)S(1)}, bf16[16,48,128]{2,1,0:T(8,128)(2,1)S(1)}, u32[]{:S(2)}, u32[]{:S(2)}) collective-permute-start(bf16[16,48,128]{2,1,0:T(8,128)(2,1)S(1)} %all_to_all.35.slots_ref), channel_id=1, source_target_pairs={{0,256},{256,0},{1,257},{257,1},{2,258},{258,2},{3,259},{259,3},{4... | collective-permute-start | bytes 589832 | tf_op jit(solution)/shard_map/ppermute | solution.py:258
  33.4 0.0 copy-start
  33.4 2.0 %copy-done = bf16[1536,1152]{1,0:T(8,128)(2,1)S(1)} copy-done((bf16[1536,1152]{1,0:T(8,128)(2,1)S(1)}, bf16[1536,1152]{1,0:T(8,128)(2,1)}, u32[]{:S(2)}) %copy-start) | copy-done | bytes 3538968
  35.4 1.1 copy-done.1
  36.4 0.3 shard_map.145
  36.7 0.0 collective-permute-done.slots_other_ref
  36.7 0.8 shard_map.146
  37.6 7.7 %collective-permute-start.1 = (bf16[8,96,256]{2,1,0:T(8,128)(2,1)S(1)}, bf16[8,96,256]{2,1,0:T(8,128)(2,1)S(1)}, u32[]{:S(2)}, u32[]{:S(2)}) collective-permute-start(bf16[8,96,256]{2,1,0:T(8,128)(2,1)S(1)} %get-tuple-element.29), channel_id=1, source_target_pairs={{0,1},{1,0},{2,3},{3,2},{4,5},{5,4},{6,7},{7,6},{8,9},{9,8},{10,11... | collective-permute-start | bytes 1179656 | tf_op jit(solution)/shard_map/ppermute | solution.py:266
  45.3 0.8 shard_map.147.one_ref
  46.1 0.6 collective-permute-done.1.two_ref
  46.6 0.1 shard_map.148
  46.7 15.2 %all_to_all.36.parts_ref = bf16[8,96,256]{2,1,0:T(8,128)(2,1)S(1)} all-to-all(bf16[8,96,256]{2,1,0:T(8,128)(2,1)S(1)} %shard_map.148), channel_id=1, replica_groups=mesh['yl'=2,'zq'=8,'zp'=2,'xy'=8,'core'=2] {'xy'}, dimensions={0} | all-to-all | bytes 786432 | tf_op jit(solution)/shard_map/all_to_all | solution.py:243
  62.0 0.1 shard_map.149
  62.0 11.4 %all_to_all.37 = bf16[8,96,256]{2,1,0:T(8,128)(2,1)S(1)} all-to-all(bf16[8,96,256]{2,1,0:T(8,128)(2,1)S(1)} %shard_map.149), channel_id=1, replica_groups=mesh['yl'=2,'zq'=8,'zp'=2,'xy'=8,'core'=2] {'xy'}, dimensions={0} | all-to-all | bytes 786432 | tf_op jit(solution)/shard_map/all_to_all | solution.py:243
  73.4 4.9 %all_gather.3.full_ref = bf16[16,96,256]{2,1,0:T(8,128)(2,1)S(1)} all-gather(bf16[8,96,256]{2,1,0:T(8,128)(2,1)S(1)} %all_to_all.37), channel_id=1, replica_groups=mesh['yl'=2,'zq'=8,'zp'=2,'xy'=8,'core'=2] {'core'}, dimensions={0}, use_global_device_ids=true | all-gather | bytes 1179648 | tf_op jit(solution)/shard_map/all_gather | solution.py:273
  78.4 0.0 copy-start.10
  78.4 0.0 copy-start.2
  78.4 1.4 shard_map.150
  79.8 8.3 %all_to_all.38.parts_ref = bf16[4,336,128]{2,1,0:T(8,128)(2,1)S(1)} all-to-all(bf16[4,336,128]{2,1,0:T(8,128)(2,1)S(1)} %shard_map.150), channel_id=1, replica_groups=mesh['yl'=2,'zq'=8,'zp'=2,'xy'=8,'core'=2] {'yl','zp'}, dimensions={0} | all-to-all | bytes 688128 | tf_op jit(solution)/shard_map/all_to_all | solution.py:243
  88.1 0.1 shard_map.151
  88.2 17.8 %all_to_all.39.parts_ref = bf16[8,48,128]{2,1,0:T(8,128)(2,1)S(1)} all-to-all(bf16[8,48,128]{2,1,0:T(8,128)(2,1)S(1)} %shard_map.151), channel_id=1, replica_groups=mesh['yl'=2,'zq'=8,'zp'=2,'xy'=8,'core'=2] {'zq'}, dimensions={0} | all-to-all | bytes 196608 | tf_op jit(solution)/shard_map/all_to_all | solution.py:243
  106.0 0.8 shard_map.152
  106.8 4.3 %all-to-all-start.5 = ((bf16[32,8,128]{2,1,0:T(8,128)(2,1)}), bf16[32,8,128]{2,1,0:T(8,128)(2,1)S(1)}, u32[]{:S(2)}, u32[]{:S(2)}) async-start(bf16[32,8,128]{2,1,0:T(8,128)(2,1)} %get-tuple-element.32), calls=%async_computation.5 | async-start | bytes 131072 | tf_op jit(solution)/shard_map/all_to_all | solution.py:243
  111.0 4.0 %collective-permute-start.2 = (bf16[40,128]{1,0:T(8,128)(2,1)S(1)}, bf16[40,128]{1,0:T(8,128)(2,1)S(1)}, u32[]{:S(2)}, u32[]{:S(2)}) collective-permute-start(bf16[40,128]{1,0:T(8,128)(2,1)S(1)} %get-tuple-element.30), channel_id=1, source_target_pairs={{0,11},{1,39},{2,65},{3,103},{4,132},{5,160},{6,206},{7,224},{8,25... | collective-permute-start | bytes 30728 | tf_op jit(solution)/shard_map/ppermute | solution.py:296
  115.1 11.9 %collective-permute-done.2.rows_ref = bf16[40,128]{1,0:T(8,128)(2,1)S(1)} collective-permute-done((bf16[40,128]{1,0:T(8,128)(2,1)S(1)}, bf16[40,128]{1,0:T(8,128)(2,1)S(1)}, u32[]{:S(2)}, u32[]{:S(2)}) %collective-permute-start.2) | collective-permute-done | bytes 10272 | tf_op jit(solution)/shard_map/ppermute | solution.py:296
  127.0 0.0 all-to-all-done.5.up_ref
  127.0 11.9 %all_to_all.40.down_ref = bf16[16,40,128]{2,1,0:T(8,128)(2,1)S(1)} all-to-all(bf16[16,40,128]{2,1,0:T(8,128)(2,1)S(1)} %shard_map.153), channel_id=1, replica_groups=mesh['yl'=2,'zq'=8,'zp'=2,'xy'=8,'core'=2] {'xy','core'}, dimensions={0} | all-to-all | bytes 327680 | tf_op jit(solution)/shard_map/all_to_all | solution.py:243
  138.9 1.1 shard_map.155
  (17 shorter events, 0.1 us)
Async XLA Ops:
  0.6 0.7 copy-start.3
  1.4 0.7 copy-start.7
  30.2 6.6 %collective-permute-start = (bf16[16,48,128]{2,1,0:T(8,128)(2,1)S(1)}, bf16[16,48,128]{2,1,0:T(8,128)(2,1)S(1)}, u32[]{:S(2)}, u32[]{:S(2)}) collective-permute-start(bf16[16,48,128]{2,1,0:T(8,128)(2,1)S(1)} %all_to_all.35.slots_ref), channel_id=1, source_target_pairs={{0,256},{256,0},{1,257},{257,1},{2,258},{258,2},{3,259},{259,3},{4... | collective-permute-start | bytes 589832 | tf_op jit(solution)/shard_map/ppermute | solution.py:258
  33.4 2.0 %copy-start = (bf16[1536,1152]{1,0:T(8,128)(2,1)S(1)}, bf16[1536,1152]{1,0:T(8,128)(2,1)}, u32[]{:S(2)}) copy-start(bf16[1536,1152]{1,0:T(8,128)(2,1)} %act_in.1) | copy-start | bytes 10616836
  35.4 1.1 copy-start.1
  37.6 9.0 %collective-permute-start.1 = (bf16[8,96,256]{2,1,0:T(8,128)(2,1)S(1)}, bf16[8,96,256]{2,1,0:T(8,128)(2,1)S(1)}, u32[]{:S(2)}, u32[]{:S(2)}) collective-permute-start(bf16[8,96,256]{2,1,0:T(8,128)(2,1)S(1)} %get-tuple-element.29), channel_id=1, source_target_pairs={{0,1},{1,0},{2,3},{3,2},{4,5},{5,4},{6,7},{7,6},{8,9},{9,8},{10,11... | collective-permute-start | bytes 1179656 | tf_op jit(solution)/shard_map/ppermute | solution.py:266
  78.3 27.6 %copy-start.4 = (f32[1,36,128]{2,0,1:T(1,128)S(1)}, f32[1,36,128]{2,0,1:T(1,128)}, u32[]{:S(2)}) copy-start(f32[1,36,128]{2,0,1:T(1,128)} %param.12) | copy-start | bytes 55300
  78.3 27.6 %copy-start.5 = (f32[1,36,128]{2,0,1:T(1,128)S(1)}, f32[1,36,128]{2,0,1:T(1,128)}, u32[]{:S(2)}) copy-start(f32[1,36,128]{2,0,1:T(1,128)} %param.13) | copy-start | bytes 55300
  78.3 27.6 %copy-start.6 = (f32[1,36,128]{2,0,1:T(1,128)S(1)}, f32[1,36,128]{2,0,1:T(1,128)}, u32[]{:S(2)}) copy-start(f32[1,36,128]{2,0,1:T(1,128)} %param.14) | copy-start | bytes 55300
  78.3 27.6 %copy-start.8 = (f32[1,6,128]{2,0,1:T(1,128)S(1)}, f32[1,6,128]{2,0,1:T(1,128)}, u32[]{:S(2)}) copy-start(f32[1,6,128]{2,0,1:T(1,128)} %param.15) | copy-start | bytes 9220
  78.4 27.6 %copy-start.9 = (f32[1,6,128]{2,0,1:T(1,128)S(1)}, f32[1,6,128]{2,0,1:T(1,128)}, u32[]{:S(2)}) copy-start(f32[1,6,128]{2,0,1:T(1,128)} %param.16) | copy-start | bytes 9220
  78.4 27.6 %copy-start.10 = (f32[1,6,128]{2,0,1:T(1,128)S(1)}, f32[1,6,128]{2,0,1:T(1,128)}, u32[]{:S(2)}) copy-start(f32[1,6,128]{2,0,1:T(1,128)} %param.17) | copy-start | bytes 9220
  78.4 36.7 %copy-start.2 = (bf16[576,192]{0,1:T(8,128)(2,1)S(1)}, bf16[576,192]{0,1:T(8,128)(2,1)}, u32[]{:S(2)}) copy-start(bf16[576,192]{0,1:T(8,128)(2,1)} %param.11) | copy-start | bytes 663556
  106.8 20.3 %all-to-all-start.5 = ((bf16[32,8,128]{2,1,0:T(8,128)(2,1)}), bf16[32,8,128]{2,1,0:T(8,128)(2,1)S(1)}, u32[]{:S(2)}, u32[]{:S(2)}) async-start(bf16[32,8,128]{2,1,0:T(8,128)(2,1)} %get-tuple-element.32), calls=%async_computation.5 | async-start | bytes 131072 | tf_op jit(solution)/shard_map/all_to_all | solution.py:243
  111.0 16.0 %collective-permute-start.2 = (bf16[40,128]{1,0:T(8,128)(2,1)S(1)}, bf16[40,128]{1,0:T(8,128)(2,1)S(1)}, u32[]{:S(2)}, u32[]{:S(2)}) collective-permute-start(bf16[40,128]{1,0:T(8,128)(2,1)S(1)} %get-tuple-element.30), channel_id=1, source_target_pairs={{0,11},{1,39},{2,65},{3,103},{4,132},{5,160},{6,206},{7,224},{8,25... | collective-permute-start | bytes 30728 | tf_op jit(solution)/shard_map/ppermute | solution.py:296

commit v4 on v3

--- a/solution.py
+++ b/solution.py
@@ -39,7 +39,7 @@
     return (master_new, first_new, second_new)
 
 
-def kernel_call(body, out_shape, n_in, scratch=(), smem=(), hbm=(), limit=32 * 2**20):
+def kernel_call(body, out_shape, n_in, scratch=(), smem=(), hbm=(), limit=12 * 2**20):
     many = isinstance(out_shape, (list, tuple))
     return pl.pallas_call(
         body,
@@ -249,7 +249,7 @@
         fetch,
         [shape(activations.shape, BF), shape(cotangent_t.shape, BF)],
         2,
-        limit=32 * 2**20,
+        limit=12 * 2**20,
     )(activations, cotangent_t)
     own = kernel_call(spread_factors, shape((N_Z, SLOT, RANK), BF), 2, [wide(SLOT)])(
         state[0], state[3]

time: 141 us -> 141 us (level)
  no operation moved by 1% of the time
where the time goes in v4:
time: 141 us; the launch traced here: 140 us
  blocking collectives  97.6 us (69%)
  starting transfers between devices  19.2 us (14%)
  waiting for transfers between devices  12.5 us (9%)
  Pallas kernels  5.48 us (4%)
  local copies, waits for them, and re-layouts  4.49 us (3%)
    all_to_all x6, blocking collectives, exchange(): return lax.all_to_all(value, axes, 0, 0, tiled=True)  92.7 us
    ppermute x1, waiting for transfers between devices, shards(): lax.ppermute(down_send, dp + mp, [(i, owner_to_base(i)) for i in range(de...  11.9 us
    ppermute x1, starting transfers between devices, shards(): other_half = lax.ppermute(other_half, 'core', [(0, 1), (1, 0)])  7.71 us
    all_gather x1, blocking collectives, shards(): full = lax.all_gather(own_half, 'core', axis=0, tiled=True)  4.9 us
    unnamed x22, local copies, waits for them, and re-layouts  4.49 us
    all_to_all x1, starting transfers between devices, exchange(): return lax.all_to_all(value, axes, 0, 0, tiled=True)  4.26 us
    ppermute x1, starting transfers between devices, shards(): lax.ppermute(down_send, dp + mp, [(i, owner_to_base(i)) for i in range(de...  4 us
    ppermute x1, starting transfers between devices, shards(): factors_other = lax.ppermute(factors, 'yl', [(0, 1), (1, 0)])  3.19 us
  transfers between devices with their start and end apart: 4, of which 2 were waited for; matrix products, arithmetic and copies ran while one was open for 0% of the time, Pallas kernels for 1%

profile of v4, /device:TPU:1, one launch (start us, length us, event | category | flops | bytes accessed | tf_op | source)
XLA Modules:
  0.0 140.0 jit_solution(8364683903706620741)
XLA Ops:
  0.6 0.0 copy-start.3
  0.6 0.7 copy-done.3
  1.4 0.7 copy-done.7
  2.1 28.1 %all_to_all.35.slots_ref = bf16[16,48,128]{2,1,0:T(8,128)(2,1)S(1)} all-to-all(bf16[16,48,128]{2,1,0:T(8,128)(2,1)S(1)} %shard_map.144), channel_id=1, replica_groups=mesh['yl'=2,'zq'=8,'zp'=2,'xy'=8,'core'=2] {'zq','zp'}, dimensions={0} | all-to-all | bytes 393216 | tf_op jit(solution)/shard_map/all_to_all | solution.py:243
  30.2 3.2 %collective-permute-start = (bf16[16,48,128]{2,1,0:T(8,128)(2,1)S(1)}, bf16[16,48,128]{2,1,0:T(8,128)(2,1)S(1)}, u32[]{:S(2)}, u32[]{:S(2)}) collective-permute-start(bf16[16,48,128]{2,1,0:T(8,128)(2,1)S(1)} %all_to_all.35.slots_ref), channel_id=1, source_target_pairs={{0,256},{256,0},{1,257},{257,1},{2,258},{258,2},{3,259},{259,3},{4... | collective-permute-start | bytes 589832 | tf_op jit(solution)/shard_map/ppermute | solution.py:258
  33.4 0.0 copy-start
  33.4 2.0 %copy-done = bf16[1536,1152]{1,0:T(8,128)(2,1)S(1)} copy-done((bf16[1536,1152]{1,0:T(8,128)(2,1)S(1)}, bf16[1536,1152]{1,0:T(8,128)(2,1)}, u32[]{:S(2)}) %copy-start) | copy-done | bytes 3538968
  35.4 1.1 copy-done.1
  36.4 0.3 shard_map.145
  36.7 0.0 collective-permute-done.slots_other_ref
  36.7 0.8 shard_map.146
  37.6 7.7 %collective-permute-start.1 = (bf16[8,96,256]{2,1,0:T(8,128)(2,1)S(1)}, bf16[8,96,256]{2,1,0:T(8,128)(2,1)S(1)}, u32[]{:S(2)}, u32[]{:S(2)}) collective-permute-start(bf16[8,96,256]{2,1,0:T(8,128)(2,1)S(1)} %get-tuple-element.29), channel_id=1, source_target_pairs={{0,1},{1,0},{2,3},{3,2},{4,5},{5,4},{6,7},{7,6},{8,9},{9,8},{10,11... | collective-permute-start | bytes 1179656 | tf_op jit(solution)/shard_map/ppermute | solution.py:266
  45.3 0.8 shard_map.147.one_ref
  46.1 0.6 collective-permute-done.1.two_ref
  46.6 0.1 shard_map.148
  46.7 15.2 %all_to_all.36.parts_ref = bf16[8,96,256]{2,1,0:T(8,128)(2,1)S(1)} all-to-all(bf16[8,96,256]{2,1,0:T(8,128)(2,1)S(1)} %shard_map.148), channel_id=1, replica_groups=mesh['yl'=2,'zq'=8,'zp'=2,'xy'=8,'core'=2] {'xy'}, dimensions={0} | all-to-all | bytes 786432 | tf_op jit(solution)/shard_map/all_to_all | solution.py:243
  62.0 0.1 shard_map.149
  62.0 11.4 %all_to_all.37 = bf16[8,96,256]{2,1,0:T(8,128)(2,1)S(1)} all-to-all(bf16[8,96,256]{2,1,0:T(8,128)(2,1)S(1)} %shard_map.149), channel_id=1, replica_groups=mesh['yl'=2,'zq'=8,'zp'=2,'xy'=8,'core'=2] {'xy'}, dimensions={0} | all-to-all | bytes 786432 | tf_op jit(solution)/shard_map/all_to_all | solution.py:243
  73.4 4.9 %all_gather.3.full_ref = bf16[16,96,256]{2,1,0:T(8,128)(2,1)S(1)} all-gather(bf16[8,96,256]{2,1,0:T(8,128)(2,1)S(1)} %all_to_all.37), channel_id=1, replica_groups=mesh['yl'=2,'zq'=8,'zp'=2,'xy'=8,'core'=2] {'core'}, dimensions={0}, use_global_device_ids=true | all-gather | bytes 1179648 | tf_op jit(solution)/shard_map/all_gather | solution.py:273
  78.4 0.0 copy-start.10
  78.4 0.0 copy-start.2
  78.4 1.4 shard_map.150
  79.8 8.3 %all_to_all.38.parts_ref = bf16[4,336,128]{2,1,0:T(8,128)(2,1)S(1)} all-to-all(bf16[4,336,128]{2,1,0:T(8,128)(2,1)S(1)} %shard_map.150), channel_id=1, replica_groups=mesh['yl'=2,'zq'=8,'zp'=2,'xy'=8,'core'=2] {'yl','zp'}, dimensions={0} | all-to-all | bytes 688128 | tf_op jit(solution)/shard_map/all_to_all | solution.py:243
  88.1 0.1 shard_map.151
  88.2 17.8 %all_to_all.39.parts_ref = bf16[8,48,128]{2,1,0:T(8,128)(2,1)S(1)} all-to-all(bf16[8,48,128]{2,1,0:T(8,128)(2,1)S(1)} %shard_map.151), channel_id=1, replica_groups=mesh['yl'=2,'zq'=8,'zp'=2,'xy'=8,'core'=2] {'zq'}, dimensions={0} | all-to-all | bytes 196608 | tf_op jit(solution)/shard_map/all_to_all | solution.py:243
  106.0 0.8 shard_map.152
  106.8 4.3 %all-to-all-start.5 = ((bf16[32,8,128]{2,1,0:T(8,128)(2,1)}), bf16[32,8,128]{2,1,0:T(8,128)(2,1)S(1)}, u32[]{:S(2)}, u32[]{:S(2)}) async-start(bf16[32,8,128]{2,1,0:T(8,128)(2,1)} %get-tuple-element.32), calls=%async_computation.5 | async-start | bytes 131072 | tf_op jit(solution)/shard_map/all_to_all | solution.py:243
  111.0 4.0 %collective-permute-start.2 = (bf16[40,128]{1,0:T(8,128)(2,1)S(1)}, bf16[40,128]{1,0:T(8,128)(2,1)S(1)}, u32[]{:S(2)}, u32[]{:S(2)}) collective-permute-start(bf16[40,128]{1,0:T(8,128)(2,1)S(1)} %get-tuple-element.30), channel_id=1, source_target_pairs={{0,11},{1,39},{2,65},{3,103},{4,132},{5,160},{6,206},{7,224},{8,25... | collective-permute-start | bytes 30728 | tf_op jit(solution)/shard_map/ppermute | solution.py:296
  115.1 11.9 %collective-permute-done.2.rows_ref = bf16[40,128]{1,0:T(8,128)(2,1)S(1)} collective-permute-done((bf16[40,128]{1,0:T(8,128)(2,1)S(1)}, bf16[40,128]{1,0:T(8,128)(2,1)S(1)}, u32[]{:S(2)}, u32[]{:S(2)}) %collective-permute-start.2) | collective-permute-done | bytes 10272 | tf_op jit(solution)/shard_map/ppermute | solution.py:296
  127.0 0.0 all-to-all-done.5.up_ref
  127.0 11.9 %all_to_all.40.down_ref = bf16[16,40,128]{2,1,0:T(8,128)(2,1)S(1)} all-to-all(bf16[16,40,128]{2,1,0:T(8,128)(2,1)S(1)} %shard_map.153), channel_id=1, replica_groups=mesh['yl'=2,'zq'=8,'zp'=2,'xy'=8,'core'=2] {'xy','core'}, dimensions={0} | all-to-all | bytes 327680 | tf_op jit(solution)/shard_map/all_to_all | solution.py:243
  138.9 1.1 shard_map.155
  (17 shorter events, 0.1 us)
Async XLA Ops:
  0.6 0.7 copy-start.3
  1.4 0.7 copy-start.7
  30.2 6.6 %collective-permute-start = (bf16[16,48,128]{2,1,0:T(8,128)(2,1)S(1)}, bf16[16,48,128]{2,1,0:T(8,128)(2,1)S(1)}, u32[]{:S(2)}, u32[]{:S(2)}) collective-permute-start(bf16[16,48,128]{2,1,0:T(8,128)(2,1)S(1)} %all_to_all.35.slots_ref), channel_id=1, source_target_pairs={{0,256},{256,0},{1,257},{257,1},{2,258},{258,2},{3,259},{259,3},{4... | collective-permute-start | bytes 589832 | tf_op jit(solution)/shard_map/ppermute | solution.py:258
  33.4 2.0 %copy-start = (bf16[1536,1152]{1,0:T(8,128)(2,1)S(1)}, bf16[1536,1152]{1,0:T(8,128)(2,1)}, u32[]{:S(2)}) copy-start(bf16[1536,1152]{1,0:T(8,128)(2,1)} %act_in.1) | copy-start | bytes 10616836
  35.4 1.1 copy-start.1
  37.6 9.0 %collective-permute-start.1 = (bf16[8,96,256]{2,1,0:T(8,128)(2,1)S(1)}, bf16[8,96,256]{2,1,0:T(8,128)(2,1)S(1)}, u32[]{:S(2)}, u32[]{:S(2)}) collective-permute-start(bf16[8,96,256]{2,1,0:T(8,128)(2,1)S(1)} %get-tuple-element.29), channel_id=1, source_target_pairs={{0,1},{1,0},{2,3},{3,2},{4,5},{5,4},{6,7},{7,6},{8,9},{9,8},{10,11... | collective-permute-start | bytes 1179656 | tf_op jit(solution)/shard_map/ppermute | solution.py:266
  78.3 27.6 %copy-start.4 = (f32[1,36,128]{2,0,1:T(1,128)S(1)}, f32[1,36,128]{2,0,1:T(1,128)}, u32[]{:S(2)}) copy-start(f32[1,36,128]{2,0,1:T(1,128)} %param.12) | copy-start | bytes 55300
  78.3 27.6 %copy-start.5 = (f32[1,36,128]{2,0,1:T(1,128)S(1)}, f32[1,36,128]{2,0,1:T(1,128)}, u32[]{:S(2)}) copy-start(f32[1,36,128]{2,0,1:T(1,128)} %param.13) | copy-start | bytes 55300
  78.3 27.6 %copy-start.6 = (f32[1,36,128]{2,0,1:T(1,128)S(1)}, f32[1,36,128]{2,0,1:T(1,128)}, u32[]{:S(2)}) copy-start(f32[1,36,128]{2,0,1:T(1,128)} %param.14) | copy-start | bytes 55300
  78.3 27.6 %copy-start.8 = (f32[1,6,128]{2,0,1:T(1,128)S(1)}, f32[1,6,128]{2,0,1:T(1,128)}, u32[]{:S(2)}) copy-start(f32[1,6,128]{2,0,1:T(1,128)} %param.15) | copy-start | bytes 9220
  78.4 27.6 %copy-start.9 = (f32[1,6,128]{2,0,1:T(1,128)S(1)}, f32[1,6,128]{2,0,1:T(1,128)}, u32[]{:S(2)}) copy-start(f32[1,6,128]{2,0,1:T(1,128)} %param.16) | copy-start | bytes 9220
  78.4 27.6 %copy-start.10 = (f32[1,6,128]{2,0,1:T(1,128)S(1)}, f32[1,6,128]{2,0,1:T(1,128)}, u32[]{:S(2)}) copy-start(f32[1,6,128]{2,0,1:T(1,128)} %param.17) | copy-start | bytes 9220
  78.4 36.7 %copy-start.2 = (bf16[576,192]{0,1:T(8,128)(2,1)S(1)}, bf16[576,192]{0,1:T(8,128)(2,1)}, u32[]{:S(2)}) copy-start(bf16[576,192]{0,1:T(8,128)(2,1)} %param.11) | copy-start | bytes 663556
  106.8 20.3 %all-to-all-start.5 = ((bf16[32,8,128]{2,1,0:T(8,128)(2,1)}), bf16[32,8,128]{2,1,0:T(8,128)(2,1)S(1)}, u32[]{:S(2)}, u32[]{:S(2)}) async-start(bf16[32,8,128]{2,1,0:T(8,128)(2,1)} %get-tuple-element.32), calls=%async_computation.5 | async-start | bytes 131072 | tf_op jit(solution)/shard_map/all_to_all | solution.py:243
  111.0 16.0 %collective-permute-start.2 = (bf16[40,128]{1,0:T(8,128)(2,1)S(1)}, bf16[40,128]{1,0:T(8,128)(2,1)S(1)}, u32[]{:S(2)}, u32[]{:S(2)}) collective-permute-start(bf16[40,128]{1,0:T(8,128)(2,1)S(1)} %get-tuple-element.30), channel_id=1, source_target_pairs={{0,11},{1,39},{2,65},{3,103},{4,132},{5,160},{6,206},{7,224},{8,25... | collective-permute-start | bytes 30728 | tf_op jit(solution)/shard_map/ppermute | solution.py:296
